TPU v7x, 32 devices: a whole 2x2x4 slice. The times are simulated.
32 devices in a mesh: parts: 2 (over x), sec: 16 (over z, y, core).
Axes of the slice: x: 2, y: 2, z: 4, core: 2. Of those that a mesh axis runs over, the one named last changes fastest.
Arguments:
- psi: bfloat16 [256, 4096], P(('parts', 'sec')), parts along dimension 0, may hold values from -6 to 6
- left_env: bfloat16 [128, 26, 4096], P(('parts', 'sec')), parts along dimension 0, may hold values from -0.75 to 0.75
- right_env: bfloat16 [128, 26, 4096], P(('parts', 'sec')), parts along dimension 0, may hold values from -0.75 to 0.75
- couple: float32 [256, 2, 26], P(('parts', 'sec')), parts along dimension 0, may hold values from -1.25 to 1.25
- left_sector: int32 [256], P(('parts', 'sec')), parts along dimension 0, may hold values from 0 to 3
- right_owner: int32 [256, 1], P(('parts', 'sec')), parts along dimension 0, may hold values from 0 to 15; in each aligned block of 8 rows (0 to 7, 8 to 15, ...) at most 2 rows name the same one
- right_local: int32 [256], P(('parts', 'sec')), parts along dimension 0, may hold values from 0 to 3
- channel: int32 [256, 2], P(('parts', 'sec')), parts along dimension 0, may hold values from 0 to 25
Outputs:
- second: float32 [256, 4096], P(('parts', 'sec')), parts along dimension 0
- direction: bfloat16 [256, 4096], P(('parts', 'sec')), parts along dimension 0
- projected: float32 [6], P('parts'), parts along dimension 0
There are 2 independent parts, one for each index of `parts`. A program takes and returns all parts, laid end to end along the dimension named above; each array names one. Nothing has to cross between parts.
Inputs may be any that keep to these rules, and one draw needn't show every extreme that they name: `right_owner`: among the 8 blocks of one device at most 2 have the same right owner.
All inputs are finite; a program needn't handle non-finite values.
Results may differ from a plain program's by a relative error of at most 0.001.
The roundings to bfloat16 on the way count: a program that leaves them out, or rounds other values in their place, can miss the bound.
Values may be sent and summed in bfloat16 or wider, within the bound.
No kernel may reach another device: no remote copies, remote signals or barrier semaphores. Data moves between devices by JAX's collectives and lax.ppermute only.
A program may use at most 128 MiB of HBM per device.

v0:
```python
import jax
import jax.numpy as jnp
from jax import lax
from jax.sharding import PartitionSpec as P

B = 64
CAP = 2


def statistics(wave, image):
    base = wave.astype(jnp.float32)
    cross, norm_wave, norm_image = lax.psum(
        (jnp.sum(base * image), jnp.sum(base * base), jnp.sum(image * image)), "sec"
    )
    theta = cross / norm_wave
    spread = norm_image - 2.0 * theta * cross + theta * theta * norm_wave
    return (theta, spread)


def per_device(psi, left_env, right_env, couple, left_sector, right_owner, right_local, channel):
    peers = lax.axis_size("sec")
    blocks = psi.shape[0]
    width = B
    terms = couple.shape[1]
    chans = couple.shape[2]
    lsecs = left_env.shape[0]
    rsecs = right_env.shape[0]
    psi = psi.reshape(blocks, width, width)
    left_env = left_env.reshape(lsecs, chans, width, width)
    count = blocks * peers * width * width

    def left_block(index):
        own_env = left_env[left_sector[index]].astype(jnp.float32)
        return jnp.einsum(
            "jw,wab->jab", couple[index], own_env, precision=lax.Precision.HIGHEST
        ).astype(jnp.bfloat16)

    lcomb = lax.map(left_block, jnp.arange(blocks, dtype=jnp.int32), batch_size=16)
    image = jnp.einsum("kjab,kbc->kajc", lcomb, psi, preferred_element_type=jnp.float32).astype(
        jnp.bfloat16
    )
    image = image.reshape(blocks, width, terms * width)
    target = right_owner[:, 0]
    position = jnp.arange(blocks, dtype=jnp.int32)
    earlier = (target[:, None] == target[None, :]) & (position[None, :] < position[:, None])
    slot = target * CAP + jnp.sum(earlier.astype(jnp.int32), axis=1)
    flat = right_local[:, None] * chans + channel
    selector = (
        flat[:, :, None] == jnp.arange(rsecs * chans, dtype=jnp.int32)[None, None, :]
    ).astype(jnp.bfloat16)
    env_rows = right_env.reshape(rsecs * chans, width, width)

    def place(values):
        empty = jnp.zeros((peers * CAP,) + values.shape[1:], values.dtype)
        return empty.at[slot].set(values).reshape((peers, CAP) + values.shape[1:])

    def unplace(values):
        return values.reshape((peers * CAP,) + values.shape[2:])[slot]

    parts = (
        lax.all_to_all(place(image), "sec", split_axis=0, concat_axis=0, tiled=True),
        lax.all_to_all(place(selector), "sec", split_axis=0, concat_axis=0, tiled=True),
    )
    sent = parts[0]
    chosen = parts[1]
    sources = sent.shape[0]
    items = sent.shape[1]
    stack = jnp.einsum(
        "scjr,rbd->scjbd", chosen, env_rows, preferred_element_type=jnp.float32
    ).astype(jnp.bfloat16)
    sent_split = sent.reshape(sources, items, width, terms, width)
    result = jnp.einsum("scajb,scjbd->scad", sent_split, stack, preferred_element_type=jnp.float32)
    hpsi_far, stack = (result, stack) + tuple(parts[2:])
    hpsi = unplace(lax.all_to_all(hpsi_far, "sec", split_axis=0, concat_axis=0, tiled=True))
    theta, spread = statistics(psi, hpsi)
    resid = hpsi - theta * psi.astype(jnp.float32)
    direction = (resid / jnp.sqrt(spread / count + 1e-06)).astype(jnp.bfloat16)
    direction_far = lax.all_to_all(place(direction), "sec", split_axis=0, concat_axis=0, tiled=True)
    sources = direction_far.shape[0]
    items = direction_far.shape[1]
    product = jnp.einsum(
        "scab,scjbd->scajd", direction_far, stack, preferred_element_type=jnp.float32
    ).astype(jnp.bfloat16)
    product = product.reshape(sources, items, width, terms * width)
    zed = unplace(lax.all_to_all(product, "sec", split_axis=0, concat_axis=0, tiled=True))
    zed_split = zed.reshape(blocks, width, terms, width)
    second = jnp.einsum("kjab,kbjd->kad", lcomb, zed_split, preferred_element_type=jnp.float32)
    dirf = direction.astype(jnp.float32)
    along, length = lax.psum((jnp.sum(dirf * second), jnp.sum(dirf * dirf)), "sec")
    projected = jnp.stack([theta, jnp.sqrt(spread / count), along / length])
    return (
        second.reshape(blocks, width * width),
        direction.reshape(blocks, width * width),
        projected,
    )


def solution(mesh):
    placed = (
        P(("parts", "sec"), None),
        P(("parts", "sec"), None, None),
        P(("parts", "sec"), None, None),
        P(("parts", "sec"), None, None),
        P(("parts", "sec")),
        P(("parts", "sec"), None),
        P(("parts", "sec")),
        P(("parts", "sec"), None),
    )
    return jax.shard_map(
        per_device,
        mesh=mesh,
        in_specs=placed,
        out_specs=(P(("parts", "sec"), None), P(("parts", "sec"), None), P("parts")),
        check_vma=False,
    )
```

profile of v0, /device:TPU:0, one launch (start us, length us, event | category | flops | bytes accessed | tf_op | source)
XLA Modules:
  0.0 184.6 jit_solution(8039333668019144000)
XLA Ops:
  0.6 0.0 copy-start
  0.6 0.9 convert_reduce_fusion
  1.6 0.7 fusion.30
  2.2 0.7 broadcast_multiply_fusion
  2.9 0.7 broadcast_add_fusion
  3.6 0.1 copy.66
  3.6 0.1 compare_convert_fusion
  3.7 0.6 broadcast_in_dim.8
  4.3 1.9 %scatter_fusion.1 = bf16[32,2,104]{2,1,0:T(2,128)(2,1)} fusion(bf16[32,2,104]{2,1,0:T(2,128)(2,1)} %broadcast_in_dim.8, s32[8]{0:T(128)S(1)} %fusion.30, bf16[8,2,104]{2,1,0:T(2,128)(2,1)S(1)} %compare_convert_fusion), kind=kCustom, calls=%fused_computation.6 | custom fusion | bytes 10016 | tf_op jit(solution)/shard_map/scatter | solution.py:55
  6.2 7.4 %all-to-all-start.1 = ((bf16[16,2,2,104]{3,2,1,0:T(2,128)(2,1)}), bf16[16,2,2,104]{3,2,1,0:T(2,128)(2,1)S(1)}, u32[]{:S(2)}, u32[]{:S(2)}) async-start(bf16[16,2,2,104]{3,2,1,0:T(2,128)(2,1)} %bitcast.10), calls=%async_computation.1 | async-start | bytes 32768 | tf_op jit(solution)/shard_map/all_to_all | solution.py:62
  13.6 2.9 %reshape.72 = bf16[4,26,64,64]{3,2,0,1:T(8,128)(2,1)S(1)} reshape(bf16[4,26,4096]{2,0,1:T(4,128)(2,1)} %param.9) | data formatting | bytes 1703936 | tf_op jit(solution)/shard_map/reshape | solution.py:29
  16.5 0.0 copy-start.1
  16.5 0.0 copy-start.4
  16.5 1.3 copy.62
  17.8 0.6 gather_fusion.1
  18.5 0.8 reshape.150
  19.3 2.7 %gather_fusion.2 = bf16[8,26,64,64]{3,2,1,0:T(8,128)(2,1)S(1)} fusion(bf16[4,26,64,64]{3,2,1,0:T(8,128)(2,1)} %copy.62, s32[8]{0:T(128)S(1)} %fusion.29), kind=kCustom, calls=%fused_computation.2 | custom fusion | bytes 3408000 | tf_op jit(solution)/shard_map/vmap()/gather | solution.py:33
  22.0 0.6 gather_fusion
  22.6 3.1 %fusion.7 = bf16[8,2,64,64]{3,1,2,0:T(2,128)(2,1)S(1)} fusion(bf16[8,26,64,64]{3,2,1,0:T(8,128)(2,1)S(1)} %gather_fusion.2, f32[8,2,26]{2,1,0:T(2,128)S(1)} %gather_fusion), kind=kOutput, calls=%fused_computation.15 | convolution fusion | flops 20512768 | bytes 1836672 | tf_op jit(solution)/shard_map/vmap(jw,wab->jab)/dot_general | solution.py:34
  25.8 0.7 copy-done.2
  26.4 0.0 copy-done.6
  26.4 0.2 fusion.10
  26.7 0.3 copy.65
  26.9 0.2 reshape.127
  27.1 0.9 broadcast_in_dim.7
  28.0 2.1 %scatter_fusion = bf16[32,64,128]{2,1,0:T(8,128)(2,1)} fusion(bf16[32,64,128]{2,1,0:T(8,128)(2,1)} %broadcast_in_dim.7, s32[8]{0:T(128)S(1)} %fusion.30, bf16[8,64,128]{2,1,0:T(8,128)(2,1)S(1)} %reshape.127), kind=kCustom, calls=%fused_computation.5 | custom fusion | bytes 393248 | tf_op jit(solution)/shard_map/scatter | solution.py:55
  30.1 0.0 all-to-all-done.1
  30.1 6.0 %all-to-all-start = ((bf16[16,2,64,128]{3,2,1,0:T(8,128)(2,1)}), bf16[16,2,64,128]{3,2,1,0:T(8,128)(2,1)S(1)}, u32[]{:S(2)}, u32[]{:S(2)}) async-start(bf16[16,2,64,128]{3,2,1,0:T(8,128)(2,1)} %bitcast.9), calls=%async_computation | async-start | bytes 1048576 | tf_op jit(solution)/shard_map/all_to_all | solution.py:61
  36.1 0.0 copy-done.5
  36.1 0.5 copy.69
  36.6 1.8 reshape.78
  38.4 1.4 fusion.4
  39.8 10.8 %all-to-all-done = bf16[16,2,64,128]{3,2,1,0:T(8,128)(2,1)S(1)} async-done(((bf16[16,2,64,128]{3,2,1,0:T(8,128)(2,1)}), bf16[16,2,64,128]{3,2,1,0:T(8,128)(2,1)S(1)}, u32[]{:S(2)}, u32[]{:S(2)}) %all-to-all-start) | async-done | bytes 524320 | tf_op jit(solution)/shard_map/all_to_all | solution.py:61
  50.6 0.4 reshape.76
  51.0 0.6 convolution_bitcast_fusion
  51.6 1.4 reshape.157
  53.0 4.1 %all-to-all-start.2 = ((f32[16,1,8192]{2,1,0:T(1,128)}), f32[16,1,8192]{2,1,0:T(1,128)S(1)}, u32[]{:S(2)}, u32[]{:S(2)}) async-start(f32[16,1,8192]{2,1,0:T(1,128)} %reshape.157), calls=%async_computation.2 | async-start | bytes 1048576 | tf_op jit(solution)/shard_map/all_to_all | solution.py:74
  57.1 0.2 reshape.73
  57.3 14.3 %all-to-all-done.2 = f32[16,1,8192]{2,1,0:T(1,128)S(1)} async-done(((f32[16,1,8192]{2,1,0:T(1,128)}), f32[16,1,8192]{2,1,0:T(1,128)S(1)}, u32[]{:S(2)}, u32[]{:S(2)}) %all-to-all-start.2) | async-done | bytes 524320 | tf_op jit(solution)/shard_map/all_to_all | solution.py:74
  71.6 0.5 broadcast.136
  72.1 1.9 %reduce.3 = f32[16,8192]{1,0:T(8,128)S(1)} reduce(f32[16,1,8192]{2,1,0:T(1,128)S(1)} %all-to-all-done.2, f32[]{:T(128)} %broadcast.136), dimensions={1}, to_apply=%all_to_all.17.reduce_sub_computation | reduce | bytes 1048580 | tf_op jit(solution)/shard_map/all_to_all | solution.py:74
  74.1 0.4 reshape.158
  74.5 0.6 gather_fusion.3
  75.0 0.1 gather.21
  75.2 0.7 multiply_reduce_fusion.1
  75.8 0.6 fusion.19
  76.5 32.7 %all-reduce.1 = (f32[]{:T(128)}, f32[]{:T(128)}, f32[]{:T(128)}) all-reduce(f32[]{:T(128)} %multiply_reduce_fusion.1, f32[]{:T(128)} %get-tuple-element.4, f32[]{:T(128)} %get-tuple-element.3), channel_id=1, replica_groups=mesh['parts'=2,'sec'=16] {'sec'}, use_global_device_ids=true, to_apply=%region_8.0 | all-reduce | flops 3 | bytes 24 | tf_op jit(solution)/shard_map/psum | solution.py:12
  112.6 0.1 broadcast_in_dim.6
  112.7 0.7 scatter_fusion.2
  113.4 0.4 reshape.159
  113.9 12.6 %all_to_all.25 = bf16[16,2,4096]{2,1,0:T(2,128)(2,1)S(1)} all-to-all(bf16[16,2,4096]{2,1,0:T(2,128)(2,1)S(1)} %reshape.159), channel_id=1, replica_groups=mesh['parts'=2,'sec'=16] {'sec'}, dimensions={0} | all-to-all | bytes 524288 | tf_op jit(solution)/shard_map/all_to_all | solution.py:78
  126.5 0.3 reshape.160
  126.8 0.5 convolution_convert_fusion
  127.4 1.1 copy.75
  128.5 1.3 reshape.81
  129.8 3.6 %all-to-all-start.4 = ((bf16[16,2,64,128]{3,2,1,0:T(8,128)(2,1)}), bf16[16,2,64,128]{3,2,1,0:T(8,128)(2,1)S(1)}, u32[]{:S(2)}, u32[]{:S(2)}) async-start(bf16[16,2,64,128]{3,2,1,0:T(8,128)(2,1)} %reshape.81), calls=%async_computation.4 | async-start | bytes 1048576 | tf_op jit(solution)/shard_map/all_to_all | solution.py:85
  133.4 1.3 multiply_reduce_fusion.2
  134.7 13.1 %all-to-all-done.4 = bf16[16,2,64,128]{3,2,1,0:T(8,128)(2,1)S(1)} async-done(((bf16[16,2,64,128]{3,2,1,0:T(8,128)(2,1)}), bf16[16,2,64,128]{3,2,1,0:T(8,128)(2,1)S(1)}, u32[]{:S(2)}, u32[]{:S(2)}) %all-to-all-start.4) | async-done | bytes 524320 | tf_op jit(solution)/shard_map/all_to_all | solution.py:85
  147.8 0.6 gather_fusion.4
  148.3 0.1 reshape.83
  148.5 0.9 multiply_reduce_fusion
  149.4 0.8 reshape.84
  150.1 32.6 %all-reduce = (f32[]{:T(128)}, f32[]{:T(128)}) all-reduce(f32[]{:T(128)} %get-tuple-element.12, f32[]{:T(128)} %get-tuple-element.10), channel_id=1, replica_groups=mesh['parts'=2,'sec'=16] {'sec'}, use_global_device_ids=true, to_apply=%region_11.0 | all-reduce | flops 2 | bytes 16 | tf_op jit(solution)/shard_map/psum | solution.py:89
  184.0 0.6 pad_maximum_fusion
  (14 shorter events, 0.1 us)
Async XLA Ops:
  0.6 21.4 %copy-start = (f32[8,2,26]{2,1,0:T(2,128)S(1)}, f32[8,2,26]{2,1,0:T(2,128)}, u32[]{:S(2)}) copy-start(f32[8,2,26]{2,1,0:T(2,128)} %param.11) | copy-start | bytes 4996
  6.2 23.9 %all-to-all-start.1 = ((bf16[16,2,2,104]{3,2,1,0:T(2,128)(2,1)}), bf16[16,2,2,104]{3,2,1,0:T(2,128)(2,1)S(1)}, u32[]{:S(2)}, u32[]{:S(2)}) async-start(bf16[16,2,2,104]{3,2,1,0:T(2,128)(2,1)} %bitcast.10), calls=%async_computation.1 | async-start | bytes 32768 | tf_op jit(solution)/shard_map/all_to_all | solution.py:62
  16.5 1.4 copy-start.1
  16.5 2.0 %copy-start.4 = (bf16[8,4096]{1,0:T(8,128)(2,1)S(1)}, bf16[8,4096]{1,0:T(8,128)(2,1)}, u32[]{:S(2)}) copy-start(bf16[8,4096]{1,0:T(8,128)(2,1)} %param.8) | copy-start | bytes 196612
  22.6 3.8 %copy-start.6 = (bf16[8,64,64,1]{2,1,0,3:T(8,128)(2,1)S(1)}, bf16[8,64,64,1]{2,1,0,3:T(8,128)(2,1)}, u32[]{:S(2)}) copy-start(bf16[8,64,64,1]{2,1,0,3:T(8,128)(2,1)} %reshape.150) | copy-start | bytes 196612
  25.7 0.7 copy-start.2
  26.4 9.7 %copy-start.5 = (bf16[4,26,4096]{2,0,1:T(4,128)(2,1)S(1)}, bf16[4,26,4096]{2,0,1:T(4,128)(2,1)}, u32[]{:S(2)}) copy-start(bf16[4,26,4096]{2,0,1:T(4,128)(2,1)} %param.10) | copy-start | bytes 2555908
  30.1 20.5 %all-to-all-start = ((bf16[16,2,64,128]{3,2,1,0:T(8,128)(2,1)}), bf16[16,2,64,128]{3,2,1,0:T(8,128)(2,1)S(1)}, u32[]{:S(2)}, u32[]{:S(2)}) async-start(bf16[16,2,64,128]{3,2,1,0:T(8,128)(2,1)} %bitcast.9), calls=%async_computation | async-start | bytes 1048576 | tf_op jit(solution)/shard_map/all_to_all | solution.py:61
  53.0 18.6 %all-to-all-start.2 = ((f32[16,1,8192]{2,1,0:T(1,128)}), f32[16,1,8192]{2,1,0:T(1,128)S(1)}, u32[]{:S(2)}, u32[]{:S(2)}) async-start(f32[16,1,8192]{2,1,0:T(1,128)} %reshape.157), calls=%async_computation.2 | async-start | bytes 1048576 | tf_op jit(solution)/shard_map/all_to_all | solution.py:74
  128.4 20.0 %copy-start.3 = (bf16[8,2,64,64]{3,1,2,0:T(2,128)(2,1)S(1)}, bf16[8,2,64,64]{3,1,2,0:T(2,128)(2,1)}, u32[]{:S(2)}) copy-start(bf16[8,2,64,64]{3,1,2,0:T(2,128)(2,1)} %copy-done.2) | copy-start | bytes 393220
  129.8 18.0 %all-to-all-start.4 = ((bf16[16,2,64,128]{3,2,1,0:T(8,128)(2,1)}), bf16[16,2,64,128]{3,2,1,0:T(8,128)(2,1)S(1)}, u32[]{:S(2)}, u32[]{:S(2)}) async-start(bf16[16,2,64,128]{3,2,1,0:T(8,128)(2,1)} %reshape.81), calls=%async_computation.4 | async-start | bytes 1048576 | tf_op jit(solution)/shard_map/all_to_all | solution.py:85
where the time goes:
time: 185 us
  blocking collectives  78 us (42%)
  waiting for transfers between devices  38.1 us (21%)
  local copies, waits for them, and re-layouts  27 us (15%)
  starting transfers between devices  21.1 us (11%)
  other arithmetic  8.16 us (4%)
  matrix products  6.65 us (4%)
  between operations  5.55 us (3%)
    psum x1, blocking collectives, statistics(): lax.psum((jnp.sum(base * image), jnp.sum(base * base), jnp.sum(image * im...  32.7 us
    psum x1, blocking collectives, per_device(): lax.psum((jnp.sum(dirf * second), jnp.sum(dirf * dirf)), 'sec')  32.6 us
    all_to_all x1, waiting for transfers between devices, per_device(): lax.all_to_all(hpsi_far, 'sec', split_axis=0, concat_axis=0, tiled=True)  14.3 us
    all_to_all x1, waiting for transfers between devices, per_device(): lax.all_to_all(product, 'sec', split_axis=0, concat_axis=0, tiled=True)  13.1 us
    all_to_all x1, blocking collectives, per_device(): lax.all_to_all(place(direction), 'sec', split_axis=0, concat_axis=0, tile...  12.6 us
    all_to_all x1, waiting for transfers between devices, per_device(): lax.all_to_all(place(image), 'sec', split_axis=0, concat_axis=0, tiled=True)  10.8 us
    all_to_all x1, starting transfers between devices, per_device(): lax.all_to_all(place(selector), 'sec', split_axis=0, concat_axis=0, tiled...  7.39 us
    all_to_all x1, starting transfers between devices, per_device(): lax.all_to_all(place(image), 'sec', split_axis=0, concat_axis=0, tiled=True)  6 us
  transfers between devices with their start and end apart: 4, of which 3 were waited for; matrix products, arithmetic and copies ran while one was open for 11% of the time, Pallas kernels for 0%

commit v1 on v0

v1 whole, which is shorter than its diff:
```python
import functools

import jax
import jax.numpy as jnp
from jax import lax
from jax.experimental import pallas as pl
from jax.experimental.pallas import tpu as pltpu
from jax.sharding import PartitionSpec as P

B = 64
CAP = 2
LANES = 128
STATS = 8
TINY = 1e-30
F32 = jnp.float32
BF16 = jnp.bfloat16


def rounded_up(value, step):
    return -(-value // step) * step


def each(count, body):
    if count <= 8:
        for i in range(count):
            body(i)
    else:
        pl.loop(0, count)(body)


def dot(a, b):
    return jnp.dot(a, b, preferred_element_type=F32)


def unroll_rows(read, stage, groups):
    def group(g):
        for t in range(B * B // LANES):
            tile = read(g, t)
            base = g * (8 * B) + 2 * t
            stage[pl.ds(base, 8, stride=B), :] = tile
            stage[pl.ds(base + 1, 8, stride=B), :] = pltpu.roll(tile, B, 1)

    each(groups, group)


def request_kernel(chans, owner, local, channel, table, slot, seen):
    blocks, terms = channel.shape

    @pl.loop(0, seen.shape[0])
    def _(p):
        seen[p] = 0

    @pl.loop(0, table.shape[0])
    def _(i):
        table[i] = 0

    def block(k):
        own = owner[k, 0]
        rank = seen[own]
        seen[own] = rank + 1
        slot[k] = own * CAP + rank
        for j in range(terms):
            table[(own * CAP + rank) * terms + j] = local[k] * chans + channel[k, j]

    each(blocks, block)


def right_kernel(env, out, stage):
    chans = env.shape[1]
    low = lax.broadcasted_iota(jnp.int32, (8, LANES), 1) < B
    rows = env[0].astype(F32)
    for g in range(-(-chans // 8)):
        height = min(8, chans - 8 * g)
        for t in range(B * B // LANES):
            tile = rows[8 * g : 8 * g + height, t * LANES : (t + 1) * LANES]
            turned = pltpu.roll(tile, B, 1)
            base = 8 * g * B + 2 * t
            stage[pl.ds(base, height, stride=B), :] = jnp.where(low[:height], tile, turned)
            stage[pl.ds(base + 1, height, stride=B), :] = jnp.where(low[:height], turned, tile)
    out[...] = stage[...].reshape(out.shape).astype(BF16)


def left_kernel(sector, couple, env, psi, lcomb, image, wave, weights, envs, stage, wave_stage):
    blocks, terms, chans = couple.shape
    lsecs = env.shape[0]
    wide = envs.shape[0]
    pitch = wide // lsecs
    rows = blocks * terms
    weights[...] = jnp.zeros_like(weights)
    envs[...] = jnp.zeros_like(envs)
    for s in range(lsecs):
        envs[s * pitch : s * pitch + chans, :] = env[s]

    def weigh(k):
        weights[pl.ds(k * terms, terms), 0:chans] = couple[k]

    each(blocks, weigh)

    def turn(k):
        place = pl.ds(k * terms, terms)
        weights[place, :] = pltpu.roll(weights[place, :], sector[k] * pitch, 1)

    each(blocks, turn)
    exact = weights[...]
    high = exact.astype(BF16)
    rest = exact - high.astype(F32)
    middle = rest.astype(BF16)
    low = (rest - middle.astype(F32)).astype(BF16)
    parts = jnp.concatenate([high, middle, low], axis=0)
    width = 512
    for n in range(B * B // width):
        sums = dot(parts, envs[:, n * width : (n + 1) * width])
        total = sums[:rows] + (sums[rows : 2 * rows] + sums[2 * rows :])
        for g in range(rows // 8):
            for t in range(width // LANES):
                tile = total[8 * g : 8 * g + 8, t * LANES : (t + 1) * LANES]
                base = 8 * g * B + 2 * (n * (width // LANES) + t)
                stage[pl.ds(base, 8, stride=B), :] = tile
                stage[pl.ds(base + 1, 8, stride=B), :] = pltpu.roll(tile, B, 1)

    def waves(g):
        held = psi[pl.ds(pl.multiple_of(8 * g, 8), 8), :].astype(F32)
        for t in range(B * B // LANES):
            tile = held[:, t * LANES : (t + 1) * LANES]
            base = 8 * g * B + 2 * t
            wave_stage[pl.ds(base, 8, stride=B), :] = tile
            wave_stage[pl.ds(base + 1, 8, stride=B), :] = pltpu.roll(tile, B, 1)

    each(blocks // 8, waves)

    def block(k):
        left = stage[pl.ds(pl.multiple_of(k * (terms * B), terms * B), terms * B), 0:B].astype(BF16)
        base = wave_stage[pl.ds(pl.multiple_of(k * B, B), B), 0:B]
        lcomb[k] = left
        wave[k] = base
        image[k] = dot(left, base.astype(BF16)).astype(BF16)

    each(blocks, block)


def gather_kernel(table, env, out):
    terms = 2

    def fill(i):
        for j in range(terms):
            out[i, :, j * B : (j + 1) * B] = env[table[i * terms + j]][:, j * B : (j + 1) * B]

    each(out.shape[0], fill)


def closed(products):
    return products[:B, :B] + pltpu.roll(products[B:, :], B, 1)[:, :B]


def image_kernel(slot, received, lcomb, image, wave, hpsi, rsel, stats, part):
    blocks = lcomb.shape[0]
    lanes = stats.shape[2]
    lane = lax.broadcasted_iota(jnp.int32, (1, lanes), 1)
    part[...] = jnp.zeros_like(part)

    def total(values):
        return jnp.sum(jnp.sum(values, axis=0, keepdims=True), axis=1, keepdims=True)

    def block(k):
        right = received[slot[k]]
        rsel[k] = right
        base = wave[k]
        h = closed(dot(image[k], right))
        hpsi[k] = h
        norm = total(base * base)
        cross = total(base * h)
        resid = h - cross / jnp.maximum(norm, TINY) * base
        zed = dot(resid.astype(BF16), right).astype(BF16)
        applied = closed(dot(lcomb[k], zed))
        sums = (
            norm,
            cross,
            total(resid * resid),
            total(resid * base),
            total(resid * applied),
            total(base * applied),
            total(resid * h),
        )
        here = lane == k
        for i, value in enumerate(sums):
            part[i : i + 1, :] = jnp.where(here, value, part[i : i + 1, :])

    each(blocks, block)
    whole = part[...]

    def spread(p):
        stats[p] = whole

    each(stats.shape[0], spread)


def second_kernel(count, stats, hpsi, wave, rsel, lcomb, second, direction, projected, stage, dir_stage):
    blocks = lcomb.shape[0]
    norm, cross, square, mixed, applied, crossed, image = (stats[:, i, :] for i in range(7))

    def total(values):
        return jnp.sum(jnp.sum(values, axis=0, keepdims=True), axis=1, keepdims=True)

    theta = total(cross) / total(norm)
    shift = theta - cross / jnp.maximum(norm, TINY)
    rr = total(square - 2.0 * shift * mixed + shift * shift * norm)
    along = total(applied - shift * (image + crossed) + shift * shift * cross)
    spread = rr / count
    projected[0] = theta[0, 0]
    projected[1] = jnp.sqrt(spread)[0, 0]
    projected[2] = (along / rr)[0, 0]
    scale = 1.0 / jnp.sqrt(spread + 1e-06)

    def block(k):
        place = pl.ds(pl.multiple_of(k * B, B), B)
        step = ((hpsi[k] - theta * wave[k]) * scale).astype(BF16)
        dir_stage[place, 0:B] = step.astype(F32)
        zed = dot(step, rsel[k]).astype(BF16)
        stage[place, 0:B] = closed(dot(lcomb[k], zed))

    each(blocks, block)
    low = lax.broadcasted_iota(jnp.int32, (8, LANES), 1) < B

    def rows(g):
        place = pl.ds(pl.multiple_of(8 * g, 8), 8)
        for t in range(B * B // LANES):
            base = 8 * g * B + 2 * t
            lanes = slice(t * LANES, (t + 1) * LANES)
            for source, target in ((stage, second), (dir_stage, direction)):
                even = source[pl.ds(base, 8, stride=B), :]
                odd = source[pl.ds(base + 1, 8, stride=B), :]
                target[place, lanes] = jnp.where(low, even, pltpu.roll(odd, B, 1)).astype(target.dtype)

    each(blocks // 8, rows)


VMEM = pl.BlockSpec(memory_space=pltpu.VMEM)
SMEM = pl.BlockSpec(memory_space=pltpu.SMEM)


def params(mib=40):
    return pltpu.CompilerParams(vmem_limit_bytes=mib << 20)


def per_device(psi, left_env, right_env, couple, left_sector, right_owner, right_local, channel):
    peers = lax.axis_size("sec")
    blocks = psi.shape[0]
    _, terms, chans = couple.shape
    lsecs = left_env.shape[0]
    rsecs = right_env.shape[0]
    slots = peers * CAP
    lanes = rounded_up(blocks, LANES)
    of = jax.ShapeDtypeStruct

    def exchange(values):
        return lax.all_to_all(values, "sec", split_axis=0, concat_axis=0, tiled=True)

    table, slot = pl.pallas_call(
        functools.partial(request_kernel, chans),
        out_shape=(of((slots * terms,), jnp.int32), of((blocks,), jnp.int32)),
        in_specs=[SMEM] * 3,
        out_specs=(SMEM, SMEM),
        scratch_shapes=[pltpu.SMEM((peers,), jnp.int32)],
        name="request",
    )(right_owner, right_local, channel)
    wanted = exchange(table.reshape(peers, CAP * terms)).reshape(slots * terms)

    right = pl.pallas_call(
        right_kernel,
        grid=(rsecs,),
        out_shape=of((rsecs * chans, B, LANES), BF16),
        in_specs=[pl.BlockSpec((1, chans, B * B), lambda s: (s, 0, 0))],
        out_specs=pl.BlockSpec((chans, B, LANES), lambda s: (s, 0, 0)),
        scratch_shapes=[pltpu.VMEM((chans * B, LANES), F32)],
        compiler_params=params(),
        cost_estimate=pl.CostEstimate(flops=10_000_000, bytes_accessed=3_000_000, transcendentals=0),
        name="right",
    )(right_env)

    wide = rounded_up(lsecs * rounded_up(chans, 32), LANES)
    lcomb, image, wave = pl.pallas_call(
        left_kernel,
        out_shape=(
            of((blocks, terms * B, B), BF16),
            of((blocks, terms * B, B), BF16),
            of((blocks, B, B), F32),
        ),
        in_specs=[SMEM, VMEM, VMEM, VMEM],
        out_specs=(VMEM, VMEM, VMEM),
        scratch_shapes=[
            pltpu.VMEM((blocks * terms, wide), F32),
            pltpu.VMEM((wide, B * B), BF16),
            pltpu.VMEM((blocks * terms * B, LANES), F32),
            pltpu.VMEM((blocks * B, LANES), F32),
        ],
        compiler_params=params(),
        cost_estimate=pl.CostEstimate(flops=100_000_000, bytes_accessed=3_000_000, transcendentals=0),
        name="left",
    )(left_sector, couple, left_env, psi)

    sent = pl.pallas_call(
        gather_kernel,
        out_shape=of((slots, B, LANES), BF16),
        in_specs=[SMEM, VMEM],
        out_specs=VMEM,
        compiler_params=params(),
        name="gather",
    )(wanted, right)
    received = exchange(sent.reshape(peers, CAP * B, LANES)).reshape(slots, B, LANES)

    hpsi, rsel, stats = pl.pallas_call(
        image_kernel,
        out_shape=(
            of((blocks, B, B), F32),
            of((blocks, B, LANES), BF16),
            of((peers, STATS, lanes), F32),
        ),
        in_specs=[SMEM] + [VMEM] * 4,
        out_specs=(VMEM, VMEM, VMEM),
        scratch_shapes=[pltpu.VMEM((STATS, lanes), F32)],
        compiler_params=params(),
        name="image",
    )(slot, received, lcomb, image, wave)
    stats = exchange(stats)

    second, direction, projected = pl.pallas_call(
        functools.partial(second_kernel, float(blocks * peers * B * B)),
        out_shape=(of((blocks, B * B), F32), of((blocks, B * B), BF16), of((3,), F32)),
        in_specs=[VMEM] * 5,
        out_specs=(VMEM, VMEM, SMEM),
        scratch_shapes=[
            pltpu.VMEM((blocks * B, LANES), F32),
            pltpu.VMEM((blocks * B, LANES), F32),
        ],
        compiler_params=params(),
        name="second",
    )(stats, hpsi, wave, rsel, lcomb)
    return second, direction, projected


def solution(mesh):
    placed = (
        P(("parts", "sec"), None),
        P(("parts", "sec"), None, None),
        P(("parts", "sec"), None, None),
        P(("parts", "sec"), None, None),
        P(("parts", "sec")),
        P(("parts", "sec"), None),
        P(("parts", "sec")),
        P(("parts", "sec"), None),
    )
    return jax.shard_map(
        per_device,
        mesh=mesh,
        in_specs=placed,
        out_specs=(P(("parts", "sec"), None), P(("parts", "sec"), None), P("parts")),
        check_vma=False,
    )
```

time: 185 us -> 58.2 us (0.31)
  blocking collectives: 78 us -> 10.8 us
  waiting for transfers between devices: 38.1 us -> 14.6 us
  local copies, waits for them, and re-layouts: 27 us -> 6.77 us
  Pallas kernels: 0 us -> 12.7 us
  starting transfers between devices: 21.1 us -> 11.4 us
  other arithmetic: 8.16 us -> 0.67 us
  matrix products: 6.65 us -> 0 us
  between operations: 5.55 us -> 0.75 us
    psum x2 -> x0, blocking collectives: 65.4 us -> none  [the longest x1 32.7 us: statistics(): lax.psum((jnp.sum(base * image), jnp.sum(base * base), jnp.sum(image * im...]
    all_to_all x4 -> x2, waiting for transfers between devices: 38.1 us -> 14.6 us  [exchange(): lax.all_to_all(values, 'sec', split_axis=0, concat_axis=0, tiled=True)]
    pallas_call x0 -> x6, Pallas kernels: none -> 12.7 us  [the longest x1 3.29 us: per_device(): pl.pallas_call(image_kernel, out_shape=(of((blocks, B, B), F32), of((bloc...]
    reshape x10 -> x1, local copies, waits for them, and re-layouts: 9.79 us -> 0.08 us  [per_device(): wanted = exchange(table.reshape(peers, CAP * terms)).reshape(slots * terms)]
    all_to_all x4 -> x2, starting transfers between devices: 21.1 us -> 11.4 us  [exchange(): lax.all_to_all(values, 'sec', split_axis=0, concat_axis=0, tiled=True)]
    dot_general x6 -> x0, matrix products: 6.65 us -> none  [the longest x1 3.11 us: left_block(): jnp.einsum('jw,wab->jab', couple[index], own_env, precision=lax.Precision...]
    gather x6 -> x0, local copies, waits for them, and re-layouts: 5.15 us -> none  [the longest x2 3.3 us: left_block(): own_env = left_env[left_sector[index]].astype(jnp.float32)]
    scatter x3 -> x0, local copies, waits for them, and re-layouts: 4.69 us -> none  [place(): return empty.at[slot].set(values).reshape((peers, CAP) + values.shape[1:])]
  transfers between devices with their start and end apart: 4 -> 2, of which waited for: 3 -> 2; matrix products, arithmetic and copies ran while one was open for 11% -> 4% of each run, Pallas kernels for 0% -> 7%
where the time goes in v1:
time: 58.2 us; the launch traced here: 57.7 us
  waiting for transfers between devices  14.6 us (25%)
  Pallas kernels  12.7 us (22%)
  starting transfers between devices  11.4 us (20%)
  blocking collectives  10.8 us (19%)
  local copies, waits for them, and re-layouts  6.77 us (12%)
  between operations  0.75 us (1%)
  other arithmetic  0.67 us (1%)
    all_to_all x2, waiting for transfers between devices, exchange(): lax.all_to_all(values, 'sec', split_axis=0, concat_axis=0, tiled=True)  14.6 us
    all_to_all x2, starting transfers between devices, exchange(): lax.all_to_all(values, 'sec', split_axis=0, concat_axis=0, tiled=True)  11.4 us
    all_to_all x1, blocking collectives, exchange(): lax.all_to_all(values, 'sec', split_axis=0, concat_axis=0, tiled=True)  10.8 us
    unnamed x14, local copies, waits for them, and re-layouts  4.83 us
    pallas_call x1, Pallas kernels, per_device(): pl.pallas_call(image_kernel, out_shape=(of((blocks, B, B), F32), of((bloc...  3.29 us
    pallas_call x1, Pallas kernels, per_device(): pl.pallas_call(right_kernel, grid=(rsecs,), out_shape=of((rsecs * chans,...  2.5 us
    pallas_call x1, Pallas kernels, per_device(): pl.pallas_call(functools.partial(request_kernel, chans), out_shape=(of((s...  1.86 us
    all_to_all x2, local copies, waits for them, and re-layouts, exchange(): lax.all_to_all(values, 'sec', split_axis=0, concat_axis=0, tiled=True)  1.85 us
  transfers between devices with their start and end apart: 2, of which 2 were waited for; matrix products, arithmetic and copies ran while one was open for 4% of the time, Pallas kernels for 7%

profile of v1, /device:TPU:0, one launch (start us, length us, event | category | flops | bytes accessed | tf_op | source)
XLA Modules:
  0.0 57.7 jit_solution(32034413410166103)
XLA Ops:
  0.6 1.3 %copy.19.owner = s32[8,1]{1,0:T(8,128)} copy(s32[8,1]{0,1:T(1,128)} %param.13) | data formatting | bytes 64 | tf_op args[5]
  2.0 1.3 %copy.20.channel = s32[8,2]{1,0:T(8,128)} copy(s32[8,2]{0,1:T(2,128)} %param.15) | data formatting | bytes 128 | tf_op args[7]
  3.3 1.9 %request.1 = (s32[64]{0:T(128)}, s32[8]{0:T(128)}) custom-call(s32[8,1]{1,0:T(8,128)} %copy.19.owner, s32[8]{0:T(128)} %local.1, s32[8,2]{1,0:T(8,128)} %copy.20.channel), custom_call_target="tpu_custom_call" | custom-call | tf_op jit(solution)/shard_map/request/pallas_call | solution.py:258
  5.2 1.3 %all_to_all.12 = s32[16,1,4]{2,0,1:T(8,128)} reshape(s32[64]{0:T(128)} %get-tuple-element.12) | data formatting | bytes 512 | tf_op jit(solution)/shard_map/all_to_all | solution.py:256
  6.5 7.4 %all-to-all-start = ((s32[16,1,4]{2,1,0:T(1,128)}), s32[16,1,4]{2,1,0:T(1,128)S(1)}, u32[]{:S(2)}, u32[]{:S(2)}) async-start(s32[16,1,4]{2,1,0:T(1,128)} %bitcast), calls=%async_computation | async-start | bytes 16384 | tf_op jit(solution)/shard_map/all_to_all | solution.py:256
  13.9 1.6 %copy.22.env = bf16[4,26,4096]{2,1,0:T(8,128)(2,1)S(1)} copy(bf16[4,26,4096]{2,0,1:T(4,128)(2,1)} %param.10) | data formatting | bytes 1703936 | tf_op args[2]
  15.6 2.5 %right.1.env = bf16[104,64,128]{2,1,0:T(8,128)(2,1)S(1)} custom-call(bf16[4,26,4096]{2,1,0:T(8,128)(2,1)S(1)} %copy.22.env), custom_call_target="tpu_custom_call" | custom-call | flops 10000000 | bytes 3000000 | tf_op jit(solution)/shard_map/right/pallas_call | solution.py:268
  18.1 0.0 copy-start.4
  18.1 2.2 %all-to-all-done = s32[16,1,4]{2,1,0:T(1,128)S(1)} async-done(((s32[16,1,4]{2,1,0:T(1,128)}), s32[16,1,4]{2,1,0:T(1,128)S(1)}, u32[]{:S(2)}, u32[]{:S(2)}) %all-to-all-start) | async-done | bytes 288 | tf_op jit(solution)/shard_map/all_to_all | solution.py:256
  20.2 0.5 broadcast.3
  20.7 0.7 %reduce.3 = s32[16,4]{1,0:T(8,128)S(1)} reduce(s32[16,1,4]{2,1,0:T(1,128)S(1)} %all-to-all-done, s32[]{:T(128)} %broadcast.3), dimensions={1}, to_apply=%all_to_all.13.reduce_sub_computation.3 | reduce | bytes 516 | tf_op jit(solution)/shard_map/all_to_all | solution.py:256
  21.4 0.1 reshape.20.table
  21.5 1.8 %gather.1 = bf16[32,64,128]{2,1,0:T(8,128)(2,1)} custom-call(s32[64]{0:T(128)S(1)} %reshape.20.table, bf16[104,64,128]{2,1,0:T(8,128)(2,1)S(1)} %right.1.env), custom_call_target="tpu_custom_call" | custom-call | tf_op jit(solution)/shard_map/gather/pallas_call | solution.py:301
  23.3 0.0 copy-start
  23.3 0.0 copy-start.1
  23.3 0.0 copy-start.2
  23.3 4.0 %all-to-all-start.1 = ((bf16[16,128,128]{2,1,0:T(8,128)(2,1)}), bf16[16,128,128]{2,1,0:T(8,128)(2,1)S(1)}, u32[]{:S(2)}, u32[]{:S(2)}) async-start(bf16[16,128,128]{2,1,0:T(8,128)(2,1)} %bitcast.1), calls=%async_computation.1 | async-start | bytes 1048576 | tf_op jit(solution)/shard_map/all_to_all | solution.py:256
  27.3 0.0 copy-done.4
  27.3 0.0 copy-start.3
  27.3 0.5 copy.23.env
  27.8 0.0 copy-done
  27.8 0.0 copy-done.1
  27.9 0.0 copy-done.2
  27.9 1.5 %left.1 = (bf16[8,128,64]{2,1,0:T(8,128)(2,1)S(1)}, bf16[8,128,64]{2,1,0:T(8,128)(2,1)S(1)}, f32[8,64,64]{2,1,0:T(8,128)S(1)}) custom-call(s32[8]{0:T(128)S(1)} %copy-done.2, f32[8,2,26]{2,1,0:T(2,128)S(1)} %copy-done.1, bf16[4,26,4096]{2,1,0:T(8,128)(2,1)S(1)} %copy.23.env, bf16[8,4096]{1,0:T(8,128)(2,1)S(1)} %copy-done), custom_call_target="tpu_custom_call" | custom-call | flops 100000000 | bytes 3000000 | tf_op jit(solution)/shard_map/left/pallas_call | solution.py:281
  29.3 12.4 %all-to-all-done.1 = bf16[16,128,128]{2,1,0:T(8,128)(2,1)S(1)} async-done(((bf16[16,128,128]{2,1,0:T(8,128)(2,1)}), bf16[16,128,128]{2,1,0:T(8,128)(2,1)S(1)}, u32[]{:S(2)}, u32[]{:S(2)}) %all-to-all-start.1) | async-done | bytes 524320 | tf_op jit(solution)/shard_map/all_to_all | solution.py:256
  41.8 0.0 copy-done.3
  41.8 3.3 %image.1 = (f32[8,64,64]{2,1,0:T(8,128)S(1)}, bf16[8,64,128]{2,1,0:T(8,128)(2,1)S(1)}, f32[16,8,128]{2,1,0:T(8,128)S(1)}) custom-call(s32[8]{0:T(128)S(1)} %copy-done.3, bf16[32,64,128]{2,1,0:T(8,128)(2,1)S(1)} %bitcast.3, bf16[8,128,64]{2,1,0:T(8,128)(2,1)S(1)} %get-tuple-element.13.lcomb, bf16[8,128,64]{2,1,0:T(8,128)(2,1)S(1)} %get-tuple-element.14.image, ...), custom_call_target="tpu_custom_call" | custom-call | tf_op jit(solution)/shard_map/image/pallas_call | solution.py:311
  45.1 10.8 %all_to_all.19.stats = f32[16,8,128]{2,1,0:T(8,128)S(1)} all-to-all(f32[16,8,128]{2,1,0:T(8,128)S(1)} %get-tuple-element.16), channel_id=1, replica_groups=mesh['parts'=2,'sec'=16] {'sec'}, dimensions={0} | all-to-all | bytes 131072 | tf_op jit(solution)/shard_map/all_to_all | solution.py:256
  55.9 1.8 %second.1 = (f32[8,4096]{1,0:T(8,128)}, bf16[8,4096]{1,0:T(8,128)(2,1)}, f32[3]{0:T(128)}) custom-call(f32[16,8,128]{2,1,0:T(8,128)S(1)} %all_to_all.19.stats, f32[8,64,64]{2,1,0:T(8,128)S(1)} %get-tuple-element.17.hpsi, f32[8,64,64]{2,1,0:T(8,128)S(1)} %get-tuple-element.15.wave, bf16[8,64,128]{2,1,0:T(8,128)(2,1)S(1)} %get-tuple-element.18.rsel, ...), custom_call_target="tpu_custom_call" | custom-call | tf_op jit(solution)/shard_map/second/pallas_call | solution.py:326
Async XLA Ops:
  6.5 13.7 %all-to-all-start = ((s32[16,1,4]{2,1,0:T(1,128)}), s32[16,1,4]{2,1,0:T(1,128)S(1)}, u32[]{:S(2)}, u32[]{:S(2)}) async-start(s32[16,1,4]{2,1,0:T(1,128)} %bitcast), calls=%async_computation | async-start | bytes 16384 | tf_op jit(solution)/shard_map/all_to_all | solution.py:256
  18.1 9.2 %copy-start.4 = (bf16[4,26,4096]{2,0,1:T(4,128)(2,1)S(1)}, bf16[4,26,4096]{2,0,1:T(4,128)(2,1)}, u32[]{:S(2)}) copy-start(bf16[4,26,4096]{2,0,1:T(4,128)(2,1)} %param.9) | copy-start | bytes 2555908
  23.3 4.5 %copy-start = (bf16[8,4096]{1,0:T(8,128)(2,1)S(1)}, bf16[8,4096]{1,0:T(8,128)(2,1)}, u32[]{:S(2)}) copy-start(bf16[8,4096]{1,0:T(8,128)(2,1)} %psi.1) | copy-start | bytes 196612
  23.3 4.5 %copy-start.1 = (f32[8,2,26]{2,1,0:T(2,128)S(1)}, f32[8,2,26]{2,1,0:T(2,128)}, u32[]{:S(2)}) copy-start(f32[8,2,26]{2,1,0:T(2,128)} %couple.1) | copy-start | bytes 4996
  23.3 4.5 %copy-start.2 = (s32[8]{0:T(128)S(1)}, s32[8]{0:T(128)}, u32[]{:S(2)}) copy-start(s32[8]{0:T(128)} %sector.1) | copy-start | bytes 100
  23.3 18.5 %all-to-all-start.1 = ((bf16[16,128,128]{2,1,0:T(8,128)(2,1)}), bf16[16,128,128]{2,1,0:T(8,128)(2,1)S(1)}, u32[]{:S(2)}, u32[]{:S(2)}) async-start(bf16[16,128,128]{2,1,0:T(8,128)(2,1)} %bitcast.1), calls=%async_computation.1 | async-start | bytes 1048576 | tf_op jit(solution)/shard_map/all_to_all | solution.py:256
  27.3 14.5 %copy-start.3 = (s32[8]{0:T(128)S(1)}, s32[8]{0:T(128)}, u32[]{:S(2)}) copy-start(s32[8]{0:T(128)} %get-tuple-element.11.slot) | copy-start | bytes 100

commit v2 on v1

--- a/solution.py
+++ b/solution.py
@@ -21,7 +21,7 @@
 
 
 def each(count, body):
-    if count <= 8:
+    if count <= 32:
         for i in range(count):
             body(i)
     else:
@@ -44,23 +44,22 @@
 
 
 def request_kernel(chans, owner, local, channel, table, slot, seen):
-    blocks, terms = channel.shape
-
-    @pl.loop(0, seen.shape[0])
-    def _(p):
+    terms, blocks = channel.shape
+
+    def clear(p):
         seen[p] = 0
-
-    @pl.loop(0, table.shape[0])
-    def _(i):
-        table[i] = 0
+        for i in range(table.shape[2]):
+            table[p, 0, i] = 0
+
+    each(seen.shape[0], clear)
 
     def block(k):
-        own = owner[k, 0]
+        own = owner[0, k]
         rank = seen[own]
         seen[own] = rank + 1
         slot[k] = own * CAP + rank
         for j in range(terms):
-            table[(own * CAP + rank) * terms + j] = local[k] * chans + channel[k, j]
+            table[own, 0, rank * terms + j] = local[k] * chans + channel[j, k]
 
     each(blocks, block)
 
@@ -139,11 +138,13 @@
 
 
 def gather_kernel(table, env, out):
-    terms = 2
-
-    def fill(i):
-        for j in range(terms):
-            out[i, :, j * B : (j + 1) * B] = env[table[i * terms + j]][:, j * B : (j + 1) * B]
+    terms = LANES // B
+
+    def fill(p):
+        for c in range(CAP):
+            for j in range(terms):
+                half = slice(j * B, (j + 1) * B)
+                out[p, c * B : (c + 1) * B, half] = env[table[p, 0, c * terms + j]][:, half]
 
     each(out.shape[0], fill)
 
@@ -257,13 +258,13 @@
 
     table, slot = pl.pallas_call(
         functools.partial(request_kernel, chans),
-        out_shape=(of((slots * terms,), jnp.int32), of((blocks,), jnp.int32)),
+        out_shape=(of((peers, 1, CAP * terms), jnp.int32), of((blocks,), jnp.int32)),
         in_specs=[SMEM] * 3,
         out_specs=(SMEM, SMEM),
         scratch_shapes=[pltpu.SMEM((peers,), jnp.int32)],
         name="request",
-    )(right_owner, right_local, channel)
-    wanted = exchange(table.reshape(peers, CAP * terms)).reshape(slots * terms)
+    )(right_owner.T, right_local, channel.T)
+    wanted = exchange(table)
 
     right = pl.pallas_call(
         right_kernel,
@@ -300,13 +301,13 @@
 
     sent = pl.pallas_call(
         gather_kernel,
-        out_shape=of((slots, B, LANES), BF16),
+        out_shape=of((peers, CAP * B, LANES), BF16),
         in_specs=[SMEM, VMEM],
         out_specs=VMEM,
         compiler_params=params(),
         name="gather",
     )(wanted, right)
-    received = exchange(sent.reshape(peers, CAP * B, LANES)).reshape(slots, B, LANES)
+    received = exchange(sent).reshape(slots, B, LANES)
 
     hpsi, rsel, stats = pl.pallas_call(
         image_kernel,

time: 58.2 us -> 52.2 us (0.90)
  local copies, waits for them, and re-layouts: 6.77 us -> 2.16 us
  other arithmetic: 0.67 us -> 0 us
  Pallas kernels: 12.7 us -> 12.1 us
    unnamed x14 -> x12, local copies, waits for them, and re-layouts: 4.83 us -> 2.16 us
    all_to_all x2 -> x0, local copies, waits for them, and re-layouts: 1.85 us -> none  [exchange(): lax.all_to_all(values, 'sec', split_axis=0, concat_axis=0, tiled=True)]
    all_to_all x1 -> x0, other arithmetic: 0.67 us -> none  [exchange(): lax.all_to_all(values, 'sec', split_axis=0, concat_axis=0, tiled=True)]
  transfers between devices with their start and end apart: 2 -> 2, of which waited for: 2 -> 2; matrix products, arithmetic and copies ran while one was open for 4% -> 4% of each run, Pallas kernels for 7% -> 8%
where the time goes in v2:
time: 52.2 us; the launch traced here: 51.8 us
  waiting for transfers between devices  14.6 us (28%)
  Pallas kernels  12.1 us (23%)
  starting transfers between devices  11.4 us (22%)
  blocking collectives  10.8 us (21%)
  local copies, waits for them, and re-layouts  2.16 us (4%)
  between operations  0.74 us (1%)
    all_to_all x2, waiting for transfers between devices, exchange(): lax.all_to_all(values, 'sec', split_axis=0, concat_axis=0, tiled=True)  14.6 us
    all_to_all x2, starting transfers between devices, exchange(): lax.all_to_all(values, 'sec', split_axis=0, concat_axis=0, tiled=True)  11.4 us
    all_to_all x1, blocking collectives, exchange(): lax.all_to_all(values, 'sec', split_axis=0, concat_axis=0, tiled=True)  10.8 us
    pallas_call x1, Pallas kernels, per_device(): pl.pallas_call(image_kernel, out_shape=(of((blocks, B, B), F32), of((bloc...  3.22 us
    pallas_call x1, Pallas kernels, per_device(): pl.pallas_call(right_kernel, grid=(rsecs,), out_shape=of((rsecs * chans,...  2.5 us
    unnamed x12, local copies, waits for them, and re-layouts  2.16 us
    pallas_call x1, Pallas kernels, per_device(): pl.pallas_call(functools.partial(second_kernel, float(blocks * peers * B...  1.82 us
    pallas_call x1, Pallas kernels, per_device(): pl.pallas_call(gather_kernel, out_shape=of((peers, CAP * B, LANES), BF16)...  1.68 us
  transfers between devices with their start and end apart: 2, of which 2 were waited for; matrix products, arithmetic and copies ran while one was open for 4% of the time, Pallas kernels for 8%

profile of v2, /device:TPU:0, one launch (start us, length us, event | category | flops | bytes accessed | tf_op | source)
XLA Modules:
  0.0 51.8 jit_solution(12619376843126684159)
XLA Ops:
  0.6 1.5 %request.1 = (s32[16,1,4]{2,1,0:T(1,128)}, s32[8]{0:T(128)}) custom-call(s32[1,8]{1,0:T(1,128)} %bitcast.5, s32[8]{0:T(128)} %local.1, s32[2,8]{1,0:T(2,128)} %bitcast.4), custom_call_target="tpu_custom_call" | custom-call | tf_op jit(solution)/shard_map/request/pallas_call | solution.py:259
  2.1 7.4 %all-to-all-start = ((s32[16,1,4]{2,1,0:T(1,128)}), s32[16,1,4]{2,1,0:T(1,128)S(1)}, u32[]{:S(2)}, u32[]{:S(2)}) async-start(s32[16,1,4]{2,1,0:T(1,128)} %get-tuple-element.12), calls=%async_computation | async-start | bytes 16384 | tf_op jit(solution)/shard_map/all_to_all | solution.py:257
  9.5 1.6 %copy.11.env = bf16[4,26,4096]{2,1,0:T(8,128)(2,1)S(1)} copy(bf16[4,26,4096]{2,0,1:T(4,128)(2,1)} %param.10) | data formatting | bytes 1703936 | tf_op args[2]
  11.2 2.5 %right.1.env = bf16[104,64,128]{2,1,0:T(8,128)(2,1)S(1)} custom-call(bf16[4,26,4096]{2,1,0:T(8,128)(2,1)S(1)} %copy.11.env), custom_call_target="tpu_custom_call" | custom-call | flops 10000000 | bytes 3000000 | tf_op jit(solution)/shard_map/right/pallas_call | solution.py:269
  13.7 0.0 copy-start.4
  13.7 2.2 %all-to-all-done.table = s32[16,1,4]{2,1,0:T(1,128)S(1)} async-done(((s32[16,1,4]{2,1,0:T(1,128)}), s32[16,1,4]{2,1,0:T(1,128)S(1)}, u32[]{:S(2)}, u32[]{:S(2)}) %all-to-all-start) | async-done | bytes 288 | tf_op jit(solution)/shard_map/all_to_all | solution.py:257
  15.8 1.7 %gather.1 = bf16[16,128,128]{2,1,0:T(8,128)(2,1)} custom-call(s32[16,1,4]{2,1,0:T(1,128)S(1)} %all-to-all-done.table, bf16[104,64,128]{2,1,0:T(8,128)(2,1)S(1)} %right.1.env), custom_call_target="tpu_custom_call" | custom-call | tf_op jit(solution)/shard_map/gather/pallas_call | solution.py:302
  17.5 0.0 copy-start
  17.5 0.0 copy-start.1
  17.5 0.0 copy-start.2
  17.5 4.0 %all-to-all-start.1 = ((bf16[16,128,128]{2,1,0:T(8,128)(2,1)}), bf16[16,128,128]{2,1,0:T(8,128)(2,1)S(1)}, u32[]{:S(2)}, u32[]{:S(2)}) async-start(bf16[16,128,128]{2,1,0:T(8,128)(2,1)} %gather.1), calls=%async_computation.1 | async-start | bytes 1048576 | tf_op jit(solution)/shard_map/all_to_all | solution.py:257
  21.5 0.0 copy-done.4
  21.5 0.0 copy-start.3
  21.5 0.5 copy.12.env
  22.0 0.0 copy-done
  22.1 0.0 copy-done.1
  22.1 0.0 copy-done.2
  22.1 1.5 %left.1 = (bf16[8,128,64]{2,1,0:T(8,128)(2,1)S(1)}, bf16[8,128,64]{2,1,0:T(8,128)(2,1)S(1)}, f32[8,64,64]{2,1,0:T(8,128)S(1)}) custom-call(s32[8]{0:T(128)S(1)} %copy-done.2, f32[8,2,26]{2,1,0:T(2,128)S(1)} %copy-done.1, bf16[4,26,4096]{2,1,0:T(8,128)(2,1)S(1)} %copy.12.env, bf16[8,4096]{1,0:T(8,128)(2,1)S(1)} %copy-done), custom_call_target="tpu_custom_call" | custom-call | flops 100000000 | bytes 3000000 | tf_op jit(solution)/shard_map/left/pallas_call | solution.py:282
  23.6 12.4 %all-to-all-done.1 = bf16[16,128,128]{2,1,0:T(8,128)(2,1)S(1)} async-done(((bf16[16,128,128]{2,1,0:T(8,128)(2,1)}), bf16[16,128,128]{2,1,0:T(8,128)(2,1)S(1)}, u32[]{:S(2)}, u32[]{:S(2)}) %all-to-all-start.1) | async-done | bytes 524320 | tf_op jit(solution)/shard_map/all_to_all | solution.py:257
  36.0 0.0 copy-done.3
  36.0 3.2 %image.1 = (f32[8,64,64]{2,1,0:T(8,128)S(1)}, bf16[8,64,128]{2,1,0:T(8,128)(2,1)S(1)}, f32[16,8,128]{2,1,0:T(8,128)S(1)}) custom-call(s32[8]{0:T(128)S(1)} %copy-done.3, bf16[32,64,128]{2,1,0:T(8,128)(2,1)S(1)} %bitcast.3, bf16[8,128,64]{2,1,0:T(8,128)(2,1)S(1)} %get-tuple-element.13.lcomb, bf16[8,128,64]{2,1,0:T(8,128)(2,1)S(1)} %get-tuple-element.14.image, ...), custom_call_target="tpu_custom_call" | custom-call | tf_op jit(solution)/shard_map/image/pallas_call | solution.py:312
  39.2 10.8 %all_to_all.15.stats = f32[16,8,128]{2,1,0:T(8,128)S(1)} all-to-all(f32[16,8,128]{2,1,0:T(8,128)S(1)} %get-tuple-element.16), channel_id=1, replica_groups=mesh['parts'=2,'sec'=16] {'sec'}, dimensions={0} | all-to-all | bytes 131072 | tf_op jit(solution)/shard_map/all_to_all | solution.py:257
  50.0 1.8 %second.1 = (f32[8,4096]{1,0:T(8,128)}, bf16[8,4096]{1,0:T(8,128)(2,1)}, f32[3]{0:T(128)}) custom-call(f32[16,8,128]{2,1,0:T(8,128)S(1)} %all_to_all.15.stats, f32[8,64,64]{2,1,0:T(8,128)S(1)} %get-tuple-element.17.hpsi, f32[8,64,64]{2,1,0:T(8,128)S(1)} %get-tuple-element.15.wave, bf16[8,64,128]{2,1,0:T(8,128)(2,1)S(1)} %get-tuple-element.18.rsel, ...), custom_call_target="tpu_custom_call" | custom-call | tf_op jit(solution)/shard_map/second/pallas_call | solution.py:327
Async XLA Ops:
  2.1 13.7 %all-to-all-start = ((s32[16,1,4]{2,1,0:T(1,128)}), s32[16,1,4]{2,1,0:T(1,128)S(1)}, u32[]{:S(2)}, u32[]{:S(2)}) async-start(s32[16,1,4]{2,1,0:T(1,128)} %get-tuple-element.12), calls=%async_computation | async-start | bytes 16384 | tf_op jit(solution)/shard_map/all_to_all | solution.py:257
  13.7 7.9 %copy-start.4 = (bf16[4,26,4096]{2,0,1:T(4,128)(2,1)S(1)}, bf16[4,26,4096]{2,0,1:T(4,128)(2,1)}, u32[]{:S(2)}) copy-start(bf16[4,26,4096]{2,0,1:T(4,128)(2,1)} %param.9) | copy-start | bytes 2555908
  17.5 4.5 %copy-start = (bf16[8,4096]{1,0:T(8,128)(2,1)S(1)}, bf16[8,4096]{1,0:T(8,128)(2,1)}, u32[]{:S(2)}) copy-start(bf16[8,4096]{1,0:T(8,128)(2,1)} %psi.1) | copy-start | bytes 196612
  17.5 4.5 %copy-start.1 = (f32[8,2,26]{2,1,0:T(2,128)S(1)}, f32[8,2,26]{2,1,0:T(2,128)}, u32[]{:S(2)}) copy-start(f32[8,2,26]{2,1,0:T(2,128)} %couple.1) | copy-start | bytes 4996
  17.5 4.6 %copy-start.2 = (s32[8]{0:T(128)S(1)}, s32[8]{0:T(128)}, u32[]{:S(2)}) copy-start(s32[8]{0:T(128)} %sector.1) | copy-start | bytes 100
  17.5 18.5 %all-to-all-start.1 = ((bf16[16,128,128]{2,1,0:T(8,128)(2,1)}), bf16[16,128,128]{2,1,0:T(8,128)(2,1)S(1)}, u32[]{:S(2)}, u32[]{:S(2)}) async-start(bf16[16,128,128]{2,1,0:T(8,128)(2,1)} %gather.1), calls=%async_computation.1 | async-start | bytes 1048576 | tf_op jit(solution)/shard_map/all_to_all | solution.py:257
  21.5 14.5 %copy-start.3 = (s32[8]{0:T(128)S(1)}, s32[8]{0:T(128)}, u32[]{:S(2)}) copy-start(s32[8]{0:T(128)} %get-tuple-element.11.slot) | copy-start | bytes 100

commit v3 on v2

v3 whole, which is shorter than its diff:
```python
import functools

import jax
import jax.numpy as jnp
from jax import lax
from jax.experimental import pallas as pl
from jax.experimental.pallas import tpu as pltpu
from jax.sharding import PartitionSpec as P

B = 64
CAP = 2
LANES = 128
TILES = B * B // LANES
STATS = 7
SPACE = 16
TINY = 1e-30
F32 = jnp.float32
BF16 = jnp.bfloat16


def rounded_up(value, step):
    return -(-value // step) * step


def each(count, body):
    if count <= 32:
        for i in range(count):
            body(i)
    else:
        pl.loop(0, count)(body)


def dot(a, b):
    return jnp.dot(a, b, preferred_element_type=F32)


def low_half(rows=8):
    return lax.broadcasted_iota(jnp.int32, (rows, LANES), 1) < B


def swap(tile):
    return pltpu.roll(tile, B, 1)


def request_kernel(rsecs, owner, local, channel, table):
    terms, blocks = channel.shape
    peers = table.shape[0]
    peer = lax.broadcasted_iota(jnp.int32, (peers, LANES), 0)
    lane = lax.broadcasted_iota(jnp.int32, (peers, LANES), 1)
    wanted = channel[...] * rsecs + local[...]
    seen = jnp.zeros((peers, LANES), jnp.int32)
    filled = jnp.zeros((peers, LANES), jnp.int32)
    for k in range(blocks):
        hit = peer == owner[:, k : k + 1]
        for j in range(terms):
            filled = jnp.where(hit & (lane == seen * terms + j), wanted[j : j + 1, k : k + 1], filled)
        seen = seen + hit.astype(jnp.int32)
    table[...] = filled[:, : table.shape[1]]


def right_kernel(env, out, stage):
    chans, rsecs, _ = env.shape
    for w in range(chans):
        rows = env[w].astype(F32)
        for t in range(TILES):
            stage[pl.ds(w * rsecs * TILES + t, rsecs, stride=TILES), :] = rows[:, t * LANES : (t + 1) * LANES]
    out[...] = stage[...].reshape(out.shape).astype(BF16)


def gather_kernel(table, env, out):
    def fill(p):
        wanted = table[pl.ds(p, 1), :]
        for i in range(table.shape[1]):
            out[p, i * TILES : (i + 1) * TILES, :] = env[wanted[0, i]]

    each(out.shape[0], fill)


def left_kernel(sector, owner, couple, env, psi, lcomb, image, wave, slot, weights, envs, stage, twice):
    blocks, terms, chans = couple.shape
    lsecs = env.shape[0]
    wide = envs.shape[0]
    pitch = wide // lsecs
    rows = blocks * terms

    own = owner[...]
    lane = lax.broadcasted_iota(jnp.int32, own.shape, 1)
    rank = jnp.zeros_like(own)
    for k in range(blocks):
        rank = rank + ((own == own[:, k : k + 1]) & (lane > k)).astype(jnp.int32)
    slot[...] = own * CAP + rank

    weights[...] = jnp.zeros_like(weights)
    envs[...] = jnp.zeros_like(envs)
    for s in range(lsecs):
        envs[s * pitch : s * pitch + chans, :] = env[s]

    def weigh(k):
        for j in range(terms):
            weights[pl.ds(j * blocks + k, 1), 0:chans] = couple[k, j : j + 1]

    each(blocks, weigh)

    def turn(k):
        for j in range(terms):
            place = pl.ds(j * blocks + k, 1)
            weights[place, :] = pltpu.roll(weights[place, :], sector[k] * pitch, 1)

    each(blocks, turn)
    exact = weights[...]
    high = exact.astype(BF16)
    rest = exact - high.astype(F32)
    middle = rest.astype(BF16)
    low = (rest - middle.astype(F32)).astype(BF16)
    parts = jnp.concatenate([high, middle, low], axis=0)
    is_low = low_half()
    width = 512
    for n in range(B * B // width):
        sums = dot(parts, envs[:, n * width : (n + 1) * width])
        total = sums[:rows] + (sums[rows : 2 * rows] + sums[2 * rows :])
        for g in range(blocks // 8):
            for t in range(width // LANES):
                lanes = slice(t * LANES, (t + 1) * LANES)
                first = total[8 * g : 8 * g + 8, lanes]
                other = total[blocks + 8 * g : blocks + 8 * g + 8, lanes]
                base = 8 * g * B + 2 * (n * (width // LANES) + t)
                stage[pl.ds(base, 8, stride=B), :] = jnp.where(is_low, first, swap(other))
                stage[pl.ds(base + 1, 8, stride=B), :] = jnp.where(is_low, swap(first), other)

    def waves(g):
        held = psi[pl.ds(pl.multiple_of(8 * g, 8), 8), :].astype(F32)
        for t in range(TILES):
            tile = held[:, t * LANES : (t + 1) * LANES]
            base = 8 * g * B + 2 * t
            twice[pl.ds(base, 8, stride=B), :] = jnp.where(is_low, tile, swap(tile))
            twice[pl.ds(base + 1, 8, stride=B), :] = jnp.where(is_low, swap(tile), tile)

    each(blocks // 8, waves)
    left_lanes = low_half(B)

    def block(k):
        place = pl.ds(pl.multiple_of(k * B, B), B)
        left = stage[place, :].astype(BF16)
        base = twice[place, :]
        lcomb[k] = left
        wave[k] = base[:, :B]
        both = jnp.concatenate([jnp.where(left_lanes, base, 0.0), jnp.where(left_lanes, 0.0, base)], axis=0)
        image[k] = dot(left, both.astype(BF16)).astype(BF16)

    each(blocks, block)


def fold(values):
    return jnp.sum(values.reshape(B // 8, 8, B), axis=0)


def image_kernel(slot, received, lcomb, image, wave, hpsi, rsel, stats, stage, resid, zed, part):
    blocks = lcomb.shape[0]
    groups = blocks // 8
    places = slot[...]

    for k in range(blocks):
        raw = received[places[0, k]].astype(F32)
        stage[pl.ds(k * 2 * B, B, stride=2), :] = raw
        stage[pl.ds(k * 2 * B + 1, B, stride=2), :] = swap(raw)

    def unfold(k):
        rsel[k] = stage[pl.ds(pl.multiple_of(k * 2 * B, 2 * B), 2 * B), 0:B].astype(BF16)

    each(blocks, unfold)

    def keep(i, k, values):
        part[i, pl.ds(pl.multiple_of(k * 8, 8), 8), :] = fold(values)

    def of_group(i, g):
        sums = part[i, pl.ds(g * 8 * 8, 8, stride=8), :]
        for s in range(1, 8):
            sums = sums + part[i, pl.ds(g * 8 * 8 + s, 8, stride=8), :]
        return jnp.sum(sums, axis=1, keepdims=True)

    def apply(k):
        h = dot(image[k], rsel[k])
        base = wave[k]
        hpsi[k] = h
        keep(0, k, base * base)
        keep(1, k, base * h)

    each(blocks, apply)

    def group(g):
        norm, cross = of_group(0, g), of_group(1, g)
        theta = cross / jnp.maximum(norm, TINY)

        for i in range(8):
            k = g * 8 + i
            h, base = hpsi[k], wave[k]
            rest = h - theta[i : i + 1, :] * base
            resid[k] = rest
            step = rest.astype(BF16)
            zed[k, 0:B] = dot(step, rsel[k, 0:B]).astype(BF16)
            zed[k, B : 2 * B] = dot(step, rsel[k, B : 2 * B]).astype(BF16)
            keep(2, k, rest * rest)
            keep(3, k, rest * base)
            keep(4, k, rest * h)

        for i in range(8):
            k = g * 8 + i
            applied = dot(lcomb[k], zed[k])
            keep(5, k, resid[k] * applied)
            keep(6, k, wave[k] * applied)

        lane = lax.broadcasted_iota(jnp.int32, (8, LANES), 1)
        packed = jnp.zeros((8, LANES), F32)
        for i, value in enumerate([norm, cross] + [of_group(i, g) for i in range(2, STATS)]):
            packed = jnp.where(lane == i, value, packed)
        spread = pltpu.roll(packed, 0, 1, stride=SPACE, stride_axis=0)
        row = jnp.sum(spread, axis=0, keepdims=True)
        if groups == 1:
            stats[...] = jnp.broadcast_to(row, stats.shape)
        else:
            pl.loop(0, stats.shape[0] // groups)(lambda p: stats.__setitem__((pl.ds(p * groups + g, 1), slice(None)), row))

    each(groups, group)


def second_kernel(count, stats, hpsi, wave, rsel, lcomb, second, direction, projected, stage, steps, zed, narrow):
    blocks = lcomb.shape[0]
    held = stats[...]
    here = lax.broadcasted_iota(jnp.int32, held.shape, 1) % SPACE == 0
    norm, cross, square, mixed, image, applied, crossed = (
        jnp.where(here, pltpu.roll(held, (LANES - i) % LANES, 1) if i else held, 0.0) for i in range(STATS)
    )

    def total(values):
        return jnp.sum(jnp.sum(values, axis=0, keepdims=True), axis=1, keepdims=True)

    theta = total(cross) / total(norm)
    shift = theta - cross / jnp.maximum(norm, TINY)
    rr = total(square - 2.0 * shift * mixed + shift * shift * norm)
    along = total(applied - shift * (image + crossed) + shift * shift * cross)
    spread = rr / count
    scale = 1.0 / jnp.sqrt(spread + 1e-06)

    def move(k):
        place = pl.ds(pl.multiple_of(k * B, B), B)
        step = ((hpsi[k] - theta * wave[k]) * scale).astype(BF16)
        narrow[k] = step
        steps[place, 0:B] = step.astype(F32)

    each(blocks, move)

    def apply(k):
        zed[k, 0:B] = dot(narrow[k], rsel[k, 0:B]).astype(BF16)
        zed[k, B : 2 * B] = dot(narrow[k], rsel[k, B : 2 * B]).astype(BF16)

    each(blocks, apply)

    def close(k):
        stage[pl.ds(pl.multiple_of(k * B, B), B), 0:B] = dot(lcomb[k], zed[k])

    each(blocks, close)
    is_low = low_half()

    def rows(g):
        place = pl.ds(pl.multiple_of(8 * g, 8), 8)
        for source, target in ((steps, direction), (stage, second)):
            for t in range(TILES):
                base = 8 * g * B + 2 * t
                even = source[pl.ds(base, 8, stride=B), :]
                odd = source[pl.ds(base + 1, 8, stride=B), :]
                target[place, t * LANES : (t + 1) * LANES] = jnp.where(is_low, even, swap(odd)).astype(target.dtype)

    each(blocks // 8, rows)
    projected[0] = theta[0, 0]
    projected[1] = jnp.sqrt(spread)[0, 0]
    projected[2] = (along / rr)[0, 0]


VMEM = pl.BlockSpec(memory_space=pltpu.VMEM)
SMEM = pl.BlockSpec(memory_space=pltpu.SMEM)


def params(mib):
    return pltpu.CompilerParams(vmem_limit_bytes=mib << 20)


def cost(flops, moved):
    return pl.CostEstimate(flops=flops, bytes_accessed=moved, transcendentals=0)


def per_device(psi, left_env, right_env, couple, left_sector, right_owner, right_local, channel):
    peers = lax.axis_size("sec")
    blocks = psi.shape[0]
    _, terms, chans = couple.shape
    lsecs = left_env.shape[0]
    rsecs = right_env.shape[0]
    slots = peers * CAP
    groups = blocks // 8
    of = jax.ShapeDtypeStruct

    def exchange(values):
        return lax.all_to_all(values, "sec", split_axis=0, concat_axis=0, tiled=True)

    owner = right_owner.T
    table = pl.pallas_call(
        functools.partial(request_kernel, rsecs),
        out_shape=of((peers, CAP * terms), jnp.int32),
        in_specs=[VMEM] * 3,
        out_specs=VMEM,
        compiler_params=params(4),
        name="request",
    )(owner, right_local.reshape(1, blocks), channel.T)
    wanted = exchange(table.reshape(peers, 1, CAP * terms)).reshape(peers, CAP * terms)

    right = pl.pallas_call(
        right_kernel,
        out_shape=of((rsecs * chans, TILES, LANES), BF16),
        in_specs=[VMEM],
        out_specs=VMEM,
        scratch_shapes=[pltpu.VMEM((rsecs * chans * TILES, LANES), F32)],
        compiler_params=params(8),
        cost_estimate=cost(10_000_000, 3_000_000),
        name="right",
    )(right_env.transpose(1, 0, 2))

    wide = rounded_up(lsecs * rounded_up(chans, 32), LANES)
    lcomb, image, wave, slot = pl.pallas_call(
        left_kernel,
        out_shape=(
            of((blocks, B, terms * B), BF16),
            of((blocks, B, terms * B), BF16),
            of((blocks, B, B), F32),
            of((1, blocks), jnp.int32),
        ),
        in_specs=[SMEM, VMEM, VMEM, VMEM, VMEM],
        out_specs=(VMEM,) * 4,
        scratch_shapes=[
            pltpu.VMEM((blocks * terms, wide), F32),
            pltpu.VMEM((wide, B * B), BF16),
            pltpu.VMEM((blocks * B, LANES), F32),
            pltpu.VMEM((blocks * B, LANES), F32),
        ],
        compiler_params=params(24),
        cost_estimate=cost(100_000_000, 3_000_000),
        name="left",
    )(left_sector, owner, couple, left_env, psi)

    sent = pl.pallas_call(
        gather_kernel,
        out_shape=of((peers, CAP * terms * TILES, LANES), BF16),
        in_specs=[VMEM, VMEM],
        out_specs=VMEM,
        compiler_params=params(8),
        name="gather",
    )(wanted, right)
    received = exchange(sent).reshape(slots, terms * TILES, LANES)

    hpsi, rsel, stats = pl.pallas_call(
        image_kernel,
        out_shape=(
            of((blocks, B, B), F32),
            of((blocks, terms * B, B), BF16),
            of((peers * groups, LANES), F32),
        ),
        in_specs=[VMEM] * 5,
        out_specs=(VMEM, VMEM, VMEM),
        scratch_shapes=[
            pltpu.VMEM((blocks * terms * B, LANES), F32),
            pltpu.VMEM((blocks, B, B), F32),
            pltpu.VMEM((blocks, terms * B, B), BF16),
            pltpu.VMEM((STATS, blocks * 8, B), F32),
        ],
        compiler_params=params(24),
        name="image",
    )(slot, received, lcomb, image, wave)
    stats = exchange(stats.reshape(peers, groups, LANES)).reshape(peers * groups, LANES)

    second, direction, projected = pl.pallas_call(
        functools.partial(second_kernel, float(blocks * peers * B * B)),
        out_shape=(of((blocks, B * B), F32), of((blocks, B * B), BF16), of((3,), F32)),
        in_specs=[VMEM] * 5,
        out_specs=(VMEM, VMEM, SMEM),
        scratch_shapes=[
            pltpu.VMEM((blocks * B, LANES), F32),
            pltpu.VMEM((blocks * B, LANES), F32),
            pltpu.VMEM((blocks, terms * B, B), BF16),
            pltpu.VMEM((blocks, B, B), BF16),
        ],
        compiler_params=params(24),
        name="second",
    )(stats, hpsi, wave, rsel, lcomb)
    return second, direction, projected


def solution(mesh):
    placed = (
        P(("parts", "sec"), None),
        P(("parts", "sec"), None, None),
        P(("parts", "sec"), None, None),
        P(("parts", "sec"), None, None),
        P(("parts", "sec")),
        P(("parts", "sec"), None),
        P(("parts", "sec")),
        P(("parts", "sec"), None),
    )
    return jax.shard_map(
        per_device,
        mesh=mesh,
        in_specs=placed,
        out_specs=(P(("parts", "sec"), None), P(("parts", "sec"), None), P("parts")),
        check_vma=False,
    )
```

time: 52.2 us -> 48.2 us (0.923)
  Pallas kernels: 12.1 us -> 6.61 us
  waiting for transfers between devices: 14.6 us -> 16.4 us
  blocking collectives: 10.8 us -> 10.2 us
    pallas_call x4, Pallas kernels: 7.11 us -> 3.98 us  [the longest x1 1.32 us: per_device(): pl.pallas_call(left_kernel, out_shape=(of((blocks, B, terms * B), BF16),...]
    pallas_call x1, Pallas kernels: 3.22 us -> 1.13 us  [per_device(): pl.pallas_call(image_kernel, out_shape=(of((blocks, B, B), F32), of((bloc...]
    all_to_all x2, waiting for transfers between devices: 14.6 us -> 16.4 us  [exchange(): lax.all_to_all(values, 'sec', split_axis=0, concat_axis=0, tiled=True)]
    all_to_all x1, blocking collectives: 10.8 us -> 10.2 us  [exchange(): lax.all_to_all(values, 'sec', split_axis=0, concat_axis=0, tiled=True)]
    unnamed x12 -> x17, local copies, waits for them, and re-layouts: 2.16 us -> 2.66 us
  transfers between devices with their start and end apart: 2 -> 2, of which waited for: 2 -> 2; matrix products, arithmetic and copies ran while one was open for 4% -> 1% of each run, Pallas kernels for 8% -> 5%
where the time goes in v3:
time: 48.2 us; the launch traced here: 47.7 us
  waiting for transfers between devices  16.4 us (34%)
  starting transfers between devices  11.1 us (23%)
  blocking collectives  10.2 us (21%)
  Pallas kernels  6.61 us (14%)
  local copies, waits for them, and re-layouts  2.66 us (6%)
  between operations  0.73 us (2%)
    all_to_all x2, waiting for transfers between devices, exchange(): lax.all_to_all(values, 'sec', split_axis=0, concat_axis=0, tiled=True)  16.4 us
    all_to_all x2, starting transfers between devices, exchange(): lax.all_to_all(values, 'sec', split_axis=0, concat_axis=0, tiled=True)  11.1 us
    all_to_all x1, blocking collectives, exchange(): lax.all_to_all(values, 'sec', split_axis=0, concat_axis=0, tiled=True)  10.2 us
    unnamed x17, local copies, waits for them, and re-layouts  2.66 us
    pallas_call x1, Pallas kernels, per_device(): pl.pallas_call(functools.partial(second_kernel, float(blocks * peers * B...  1.51 us
    pallas_call x1, Pallas kernels, per_device(): pl.pallas_call(left_kernel, out_shape=(of((blocks, B, terms * B), BF16),...  1.32 us
    pallas_call x1, Pallas kernels, per_device(): pl.pallas_call(image_kernel, out_shape=(of((blocks, B, B), F32), of((bloc...  1.13 us
    pallas_call x1, Pallas kernels, per_device(): pl.pallas_call(right_kernel, out_shape=of((rsecs * chans, TILES, LANES),...  0.98 us
  transfers between devices with their start and end apart: 2, of which 2 were waited for; matrix products, arithmetic and copies ran while one was open for 1% of the time, Pallas kernels for 5%

profile of v3, /device:TPU:0, one launch (start us, length us, event | category | flops | bytes accessed | tf_op | source)
XLA Modules:
  0.0 47.7 jit_solution(1493529198248469402)
XLA Ops:
  0.6 0.0 copy-start.6
  0.6 0.0 copy-start.3
  0.7 0.0 copy-start.4
  0.7 0.6 %copy-done.6 = s32[8]{0:T(128)S(1)} copy-done((s32[8]{0:T(128)S(1)}, s32[8]{0:T(128)}, u32[]{:S(2)}) %copy-start.6) | copy-done | bytes 56
  1.3 0.0 copy-done.3
  1.3 0.0 copy-done.4
  1.3 0.7 %request.1 = s32[16,4]{1,0:T(8,128)} custom-call(s32[1,8]{1,0:T(1,128)S(1)} %bitcast.18, s32[1,8]{1,0:T(1,128)S(1)} %bitcast.21, s32[2,8]{1,0:T(2,128)S(1)} %bitcast.20), custom_call_target="tpu_custom_call" | custom-call | tf_op jit(solution)/shard_map/request/pallas_call | solution.py:305
  2.1 7.4 %all-to-all-start = ((s32[16,1,4]{2,1,0:T(1,128)}), s32[16,1,4]{2,1,0:T(1,128)S(1)}, u32[]{:S(2)}, u32[]{:S(2)}) async-start(s32[16,1,4]{2,1,0:T(1,128)} %bitcast.10), calls=%async_computation | async-start | bytes 16384 | tf_op jit(solution)/shard_map/all_to_all | solution.py:302
  9.5 0.0 copy-start
  9.5 1.1 %copy-done = bf16[4,26,4096]{2,0,1:T(4,128)(2,1)S(1)} copy-done((bf16[4,26,4096]{2,0,1:T(4,128)(2,1)S(1)}, bf16[4,26,4096]{2,0,1:T(4,128)(2,1)}, u32[]{:S(2)}) %copy-start) | copy-done | bytes 851992
  10.6 1.0 %right.1.env = bf16[104,32,128]{2,1,0:T(8,128)(2,1)S(1)} custom-call(bf16[26,4,4096]{2,1,0:T(4,128)(2,1)S(1)} %bitcast.14), custom_call_target="tpu_custom_call" | custom-call | flops 10000000 | bytes 3000000 | tf_op jit(solution)/shard_map/right/pallas_call | solution.py:315
  11.6 4.2 %all-to-all-done = s32[16,1,4]{2,1,0:T(1,128)S(1)} async-done(((s32[16,1,4]{2,1,0:T(1,128)}), s32[16,1,4]{2,1,0:T(1,128)S(1)}, u32[]{:S(2)}, u32[]{:S(2)}) %all-to-all-start) | async-done | bytes 288 | tf_op jit(solution)/shard_map/all_to_all | solution.py:302
  15.8 1.0 %gather.1 = bf16[16,128,128]{2,1,0:T(8,128)(2,1)} custom-call(s32[16,4]{1,0:T(8,128)S(1)} %bitcast.15, bf16[104,32,128]{2,1,0:T(8,128)(2,1)S(1)} %right.1.env), custom_call_target="tpu_custom_call" | custom-call | tf_op jit(solution)/shard_map/gather/pallas_call | solution.py:348
  16.7 0.0 copy-start.7
  16.7 3.7 %all-to-all-start.1 = ((bf16[16,128,128]{2,1,0:T(8,128)(2,1)}), bf16[16,128,128]{2,1,0:T(8,128)(2,1)S(1)}, u32[]{:S(2)}, u32[]{:S(2)}) async-start(bf16[16,128,128]{2,1,0:T(8,128)(2,1)} %gather.1), calls=%async_computation.1 | async-start | bytes 1048576 | tf_op jit(solution)/shard_map/all_to_all | solution.py:302
  20.5 0.0 copy-done.7
  20.5 0.0 copy-start.1
  20.5 0.0 copy-start.2
  20.5 0.0 copy-start.5
  20.5 0.5 %copy.14.env = bf16[4,26,4096]{2,1,0:T(8,128)(2,1)S(1)} copy(bf16[4,26,4096]{2,0,1:T(4,128)(2,1)S(1)} %copy-done.7) | data formatting | bytes 1703936 | tf_op args[1]
  21.0 0.3 copy-done.1
  21.3 0.0 copy-done.2
  21.3 0.0 copy-done.5
  21.3 1.3 %left.1 = (bf16[8,64,128]{2,1,0:T(8,128)(2,1)S(1)}, bf16[8,64,128]{2,1,0:T(8,128)(2,1)S(1)}, f32[8,64,64]{2,1,0:T(8,128)S(1)}, s32[1,8]{1,0:T(1,128)S(1)}) custom-call(s32[8]{0:T(128)S(1)} %copy-done.5, s32[1,8]{1,0:T(1,128)S(1)} %bitcast.19, f32[8,2,26]{2,1,0:T(2,128)S(1)} %copy-done.2, bf16[4,26,4096]{2,1,0:T(8,128)(2,1)S(1)} %copy.14.env, ...), custom_call_target="tpu_custom_call" | custom-call | flops 100000000 | bytes 3000000 | tf_op jit(solution)/shard_map/left/pallas_call | solution.py:327
  22.6 12.2 %all-to-all-done.1 = bf16[16,128,128]{2,1,0:T(8,128)(2,1)S(1)} async-done(((bf16[16,128,128]{2,1,0:T(8,128)(2,1)}), bf16[16,128,128]{2,1,0:T(8,128)(2,1)S(1)}, u32[]{:S(2)}, u32[]{:S(2)}) %all-to-all-start.1) | async-done | bytes 524320 | tf_op jit(solution)/shard_map/all_to_all | solution.py:302
  34.9 1.1 %image.1 = (f32[8,64,64]{2,1,0:T(8,128)S(1)}, bf16[8,128,64]{2,1,0:T(8,128)(2,1)S(1)}, f32[16,128]{1,0:T(8,128)S(1)}) custom-call(s32[1,8]{1,0:T(1,128)S(1)} %get-tuple-element.10.slot, bf16[32,64,128]{2,1,0:T(8,128)(2,1)S(1)} %bitcast.13, bf16[8,64,128]{2,1,0:T(8,128)(2,1)S(1)} %get-tuple-element.11.lcomb, bf16[8,64,128]{2,1,0:T(8,128)(2,1)S(1)} %get-tuple-element.12.image, ...), custom_call_target="tpu_custom_call" | custom-call | tf_op jit(solution)/shard_map/image/pallas_call | solution.py:358
  36.0 10.2 %all_to_all.15 = f32[16,1,128]{2,1,0:T(1,128)S(1)} all-to-all(f32[16,1,128]{2,1,0:T(1,128)S(1)} %bitcast.17), channel_id=1, replica_groups=mesh['parts'=2,'sec'=16] {'sec'}, dimensions={0} | all-to-all | bytes 16384 | tf_op jit(solution)/shard_map/all_to_all | solution.py:302
  46.2 1.5 %second.1 = (f32[8,4096]{1,0:T(8,128)}, bf16[8,4096]{1,0:T(8,128)(2,1)}, f32[3]{0:T(128)}) custom-call(f32[16,128]{1,0:T(8,128)S(1)} %bitcast.16, f32[8,64,64]{2,1,0:T(8,128)S(1)} %get-tuple-element.15.hpsi, f32[8,64,64]{2,1,0:T(8,128)S(1)} %get-tuple-element.13.wave, bf16[8,128,64]{2,1,0:T(8,128)(2,1)S(1)} %get-tuple-element.16.rsel, ...), custom_call_target="tpu_custom_call" | custom-call | tf_op jit(solution)/shard_map/second/pallas_call | solution.py:378
Async XLA Ops:
  0.6 0.7 %copy-start.6 = (s32[8]{0:T(128)S(1)}, s32[8]{0:T(128)}, u32[]{:S(2)}) copy-start(s32[8]{0:T(128)} %param.14) | copy-start | bytes 100
  0.6 0.7 %copy-start.3 = (s32[8,1]{0,1:T(1,128)S(1)}, s32[8,1]{0,1:T(1,128)}, u32[]{:S(2)}) copy-start(s32[8,1]{0,1:T(1,128)} %param.13) | copy-start | bytes 100
  0.7 0.7 %copy-start.4 = (s32[8,2]{0,1:T(2,128)S(1)}, s32[8,2]{0,1:T(2,128)}, u32[]{:S(2)}) copy-start(s32[8,2]{0,1:T(2,128)} %param.15) | copy-start | bytes 196
  2.1 13.7 %all-to-all-start = ((s32[16,1,4]{2,1,0:T(1,128)}), s32[16,1,4]{2,1,0:T(1,128)S(1)}, u32[]{:S(2)}, u32[]{:S(2)}) async-start(s32[16,1,4]{2,1,0:T(1,128)} %bitcast.10), calls=%async_computation | async-start | bytes 16384 | tf_op jit(solution)/shard_map/all_to_all | solution.py:302
  9.5 1.2 %copy-start = (bf16[4,26,4096]{2,0,1:T(4,128)(2,1)S(1)}, bf16[4,26,4096]{2,0,1:T(4,128)(2,1)}, u32[]{:S(2)}) copy-start(bf16[4,26,4096]{2,0,1:T(4,128)(2,1)} %param.10) | copy-start | bytes 2555908
  16.7 3.7 %copy-start.7 = (bf16[4,26,4096]{2,0,1:T(4,128)(2,1)S(1)}, bf16[4,26,4096]{2,0,1:T(4,128)(2,1)}, u32[]{:S(2)}) copy-start(bf16[4,26,4096]{2,0,1:T(4,128)(2,1)} %param.9) | copy-start | bytes 2555908
  16.7 18.1 %all-to-all-start.1 = ((bf16[16,128,128]{2,1,0:T(8,128)(2,1)}), bf16[16,128,128]{2,1,0:T(8,128)(2,1)S(1)}, u32[]{:S(2)}, u32[]{:S(2)}) async-start(bf16[16,128,128]{2,1,0:T(8,128)(2,1)} %gather.1), calls=%async_computation.1 | async-start | bytes 1048576 | tf_op jit(solution)/shard_map/all_to_all | solution.py:302
  20.5 0.8 %copy-start.1 = (bf16[8,4096]{1,0:T(8,128)(2,1)S(1)}, bf16[8,4096]{1,0:T(8,128)(2,1)}, u32[]{:S(2)}) copy-start(bf16[8,4096]{1,0:T(8,128)(2,1)} %psi.1) | copy-start | bytes 196612
  20.5 0.8 %copy-start.2 = (f32[8,2,26]{2,1,0:T(2,128)S(1)}, f32[8,2,26]{2,1,0:T(2,128)}, u32[]{:S(2)}) copy-start(f32[8,2,26]{2,1,0:T(2,128)} %couple.1) | copy-start | bytes 4996
  20.5 0.8 %copy-start.5 = (s32[8]{0:T(128)S(1)}, s32[8]{0:T(128)}, u32[]{:S(2)}) copy-start(s32[8]{0:T(128)} %sector.1) | copy-start | bytes 100

commit v4 on v3

--- a/solution.py
+++ b/solution.py
@@ -14,6 +14,9 @@
 STATS = 7
 SPACE = 16
 TINY = 1e-30
+TABLE_ORDER = (9, 11, 12, 15, 0, 14, 6, 1, 8, 3, 4, 10, 7, 5, 13, 2)
+MATRIX_ORDER = (9, 11, 5, 15, 12, 8, 6, 1, 10, 3, 4, 14, 7, 0, 13, 2)
+SUM_ORDER = (9, 6, 0, 3, 11, 2, 4, 14, 1, 10, 12, 15, 8, 7, 13, 5)
 F32 = jnp.float32
 BF16 = jnp.bfloat16
 
@@ -30,6 +33,25 @@
         pl.loop(0, count)(body)
 
 
+def run_of(order, peers):
+    return 0 if peers % len(order) else peers // len(order)
+
+
+def listed(order, peers):
+    run = run_of(order, peers)
+    return [q * run + i for q in order for i in range(run)] if run else list(range(peers))
+
+
+def replaced(values, pairs, run):
+    if not run:
+        return values
+    whole = values // run if run > 1 else values
+    moved = values
+    for old, new in pairs:
+        moved = jnp.where(whole == old, values + (new - old) * run, moved)
+    return moved
+
+
 def dot(a, b):
     return jnp.dot(a, b, preferred_element_type=F32)
 
@@ -46,6 +68,7 @@
     terms, blocks = channel.shape
     peers = table.shape[0]
     peer = lax.broadcasted_iota(jnp.int32, (peers, LANES), 0)
+    peer = replaced(peer, enumerate(TABLE_ORDER), run_of(TABLE_ORDER, peers))
     lane = lax.broadcasted_iota(jnp.int32, (peers, LANES), 1)
     wanted = channel[...] * rsecs + local[...]
     seen = jnp.zeros((peers, LANES), jnp.int32)
@@ -68,15 +91,20 @@
 
 
 def gather_kernel(table, env, out):
-    def fill(p):
-        wanted = table[pl.ds(p, 1), :]
-        for i in range(table.shape[1]):
-            out[p, i * TILES : (i + 1) * TILES, :] = env[wanted[0, i]]
-
-    each(out.shape[0], fill)
-
-
-def left_kernel(sector, owner, couple, env, psi, lcomb, image, wave, slot, weights, envs, stage, twice):
+    peers = out.shape[0]
+    run = run_of(MATRIX_ORDER, peers)
+    starts = [(q * run, TABLE_ORDER.index(peer) * run) for q, peer in enumerate(MATRIX_ORDER)] if run else [(0, 0)]
+    for target, source in starts:
+
+        def fill(p):
+            wanted = table[pl.ds(source + p, 1), :]
+            for i in range(table.shape[1]):
+                out[target + p, i * TILES : (i + 1) * TILES, :] = env[wanted[0, i]]
+
+        each(run or peers, fill)
+
+
+def left_kernel(peers, sector, owner, couple, env, psi, lcomb, image, wave, slot, weights, envs, stage, twice):
     blocks, terms, chans = couple.shape
     lsecs = env.shape[0]
     wide = envs.shape[0]
@@ -88,7 +116,8 @@
     rank = jnp.zeros_like(own)
     for k in range(blocks):
         rank = rank + ((own == own[:, k : k + 1]) & (lane > k)).astype(jnp.int32)
-    slot[...] = own * CAP + rank
+    place = [(peer, q) for q, peer in enumerate(MATRIX_ORDER)]
+    slot[...] = replaced(own, place, run_of(MATRIX_ORDER, peers)) * CAP + rank
 
     weights[...] = jnp.zeros_like(weights)
     envs[...] = jnp.zeros_like(envs)
@@ -298,8 +327,9 @@
     groups = blocks // 8
     of = jax.ShapeDtypeStruct
 
-    def exchange(values):
-        return lax.all_to_all(values, "sec", split_axis=0, concat_axis=0, tiled=True)
+    def exchange(values, order):
+        members = [listed(order, peers)]
+        return lax.all_to_all(values, "sec", split_axis=0, concat_axis=0, axis_index_groups=members, tiled=True)
 
     owner = right_owner.T
     table = pl.pallas_call(
@@ -310,7 +340,7 @@
         compiler_params=params(4),
         name="request",
     )(owner, right_local.reshape(1, blocks), channel.T)
-    wanted = exchange(table.reshape(peers, 1, CAP * terms)).reshape(peers, CAP * terms)
+    wanted = exchange(table.reshape(peers, 1, CAP * terms), TABLE_ORDER).reshape(peers, CAP * terms)
 
     right = pl.pallas_call(
         right_kernel,
@@ -325,7 +355,7 @@
 
     wide = rounded_up(lsecs * rounded_up(chans, 32), LANES)
     lcomb, image, wave, slot = pl.pallas_call(
-        left_kernel,
+        functools.partial(left_kernel, peers),
         out_shape=(
             of((blocks, B, terms * B), BF16),
             of((blocks, B, terms * B), BF16),
@@ -353,7 +383,7 @@
         compiler_params=params(8),
         name="gather",
     )(wanted, right)
-    received = exchange(sent).reshape(slots, terms * TILES, LANES)
+    received = exchange(sent, MATRIX_ORDER).reshape(slots, terms * TILES, LANES)
 
     hpsi, rsel, stats = pl.pallas_call(
         image_kernel,
@@ -373,7 +403,7 @@
         compiler_params=params(24),
         name="image",
     )(slot, received, lcomb, image, wave)
-    stats = exchange(stats.reshape(peers, groups, LANES)).reshape(peers * groups, LANES)
+    stats = exchange(stats.reshape(peers, groups, LANES), SUM_ORDER).reshape(peers * groups, LANES)
 
     second, direction, projected = pl.pallas_call(
         functools.partial(second_kernel, float(blocks * peers * B * B)),

time: 48.2 us -> 43 us (0.89)
  waiting for transfers between devices: 16.4 us -> 12 us
  blocking collectives: 10.2 us -> 8.57 us
  starting transfers between devices: 11.1 us -> 12 us
    all_to_all x2, waiting for transfers between devices: 16.4 us -> 12 us  [exchange(): lax.all_to_all(values, 'sec', split_axis=0, concat_axis=0, axis_index_gro...]
    all_to_all x1, blocking collectives: 10.2 us -> 8.57 us  [exchange(): lax.all_to_all(values, 'sec', split_axis=0, concat_axis=0, axis_index_gro...]
    all_to_all x2, starting transfers between devices: 11.1 us -> 12 us  [exchange(): lax.all_to_all(values, 'sec', split_axis=0, concat_axis=0, axis_index_gro...]
where the time goes in v4:
time: 43 us; the launch traced here: 42.6 us
  starting transfers between devices  12 us (28%)
  waiting for transfers between devices  12 us (28%)
  blocking collectives  8.57 us (20%)
  Pallas kernels  6.61 us (15%)
  local copies, waits for them, and re-layouts  2.66 us (6%)
  between operations  0.71 us (2%)
    all_to_all x2, waiting for transfers between devices, exchange(): lax.all_to_all(values, 'sec', split_axis=0, concat_axis=0, axis_index_gro...  12 us
    all_to_all x2, starting transfers between devices, exchange(): lax.all_to_all(values, 'sec', split_axis=0, concat_axis=0, axis_index_gro...  12 us
    all_to_all x1, blocking collectives, exchange(): lax.all_to_all(values, 'sec', split_axis=0, concat_axis=0, axis_index_gro...  8.57 us
    unnamed x17, local copies, waits for them, and re-layouts  2.66 us
    pallas_call x1, Pallas kernels, per_device(): pl.pallas_call(functools.partial(second_kernel, float(blocks * peers * B...  1.51 us
    pallas_call x1, Pallas kernels, per_device(): pl.pallas_call(functools.partial(left_kernel, peers), out_shape=(of((bloc...  1.33 us
    pallas_call x1, Pallas kernels, per_device(): pl.pallas_call(image_kernel, out_shape=(of((blocks, B, B), F32), of((bloc...  1.13 us
    pallas_call x1, Pallas kernels, per_device(): pl.pallas_call(right_kernel, out_shape=of((rsecs * chans, TILES, LANES),...  0.98 us
  transfers between devices with their start and end apart: 2, of which 2 were waited for; matrix products, arithmetic and copies ran while one was open for 1% of the time, Pallas kernels for 5%

profile of v4, /device:TPU:0, one launch (start us, length us, event | category | flops | bytes accessed | tf_op | source)
XLA Modules:
  0.0 42.6 jit_solution(3951207926206825986)
XLA Ops:
  0.6 0.0 copy-start.6
  0.6 0.0 copy-start.3
  0.7 0.0 copy-start.4
  0.7 0.6 %copy-done.6 = s32[8]{0:T(128)S(1)} copy-done((s32[8]{0:T(128)S(1)}, s32[8]{0:T(128)}, u32[]{:S(2)}) %copy-start.6) | copy-done | bytes 56
  1.3 0.0 copy-done.3
  1.3 0.0 copy-done.4
  1.3 0.7 %request.1 = s32[16,4]{1,0:T(8,128)} custom-call(s32[1,8]{1,0:T(1,128)S(1)} %bitcast.18, s32[1,8]{1,0:T(1,128)S(1)} %bitcast.21, s32[2,8]{1,0:T(2,128)S(1)} %bitcast.20), custom_call_target="tpu_custom_call" | custom-call | tf_op jit(solution)/shard_map/request/pallas_call | solution.py:335
  2.1 7.6 %all-to-all-start = ((s32[16,1,4]{2,1,0:T(1,128)}), s32[16,1,4]{2,1,0:T(1,128)S(1)}, u32[]{:S(2)}, u32[]{:S(2)}) async-start(s32[16,1,4]{2,1,0:T(1,128)} %bitcast.10), calls=%async_computation | async-start | bytes 16384 | tf_op jit(solution)/shard_map/all_to_all | solution.py:332
  9.6 0.0 copy-start
  9.6 1.1 %copy-done = bf16[4,26,4096]{2,0,1:T(4,128)(2,1)S(1)} copy-done((bf16[4,26,4096]{2,0,1:T(4,128)(2,1)S(1)}, bf16[4,26,4096]{2,0,1:T(4,128)(2,1)}, u32[]{:S(2)}) %copy-start) | copy-done | bytes 851992
  10.8 1.0 %right.1.env = bf16[104,32,128]{2,1,0:T(8,128)(2,1)S(1)} custom-call(bf16[26,4,4096]{2,1,0:T(4,128)(2,1)S(1)} %bitcast.14), custom_call_target="tpu_custom_call" | custom-call | flops 10000000 | bytes 3000000 | tf_op jit(solution)/shard_map/right/pallas_call | solution.py:345
  11.8 2.0 %all-to-all-done = s32[16,1,4]{2,1,0:T(1,128)S(1)} async-done(((s32[16,1,4]{2,1,0:T(1,128)}), s32[16,1,4]{2,1,0:T(1,128)S(1)}, u32[]{:S(2)}, u32[]{:S(2)}) %all-to-all-start) | async-done | bytes 288 | tf_op jit(solution)/shard_map/all_to_all | solution.py:332
  13.7 1.0 %gather.1 = bf16[16,128,128]{2,1,0:T(8,128)(2,1)} custom-call(s32[16,4]{1,0:T(8,128)S(1)} %bitcast.15, bf16[104,32,128]{2,1,0:T(8,128)(2,1)S(1)} %right.1.env), custom_call_target="tpu_custom_call" | custom-call | tf_op jit(solution)/shard_map/gather/pallas_call | solution.py:378
  14.7 0.0 copy-start.7
  14.7 4.4 %all-to-all-start.1 = ((bf16[16,128,128]{2,1,0:T(8,128)(2,1)}), bf16[16,128,128]{2,1,0:T(8,128)(2,1)S(1)}, u32[]{:S(2)}, u32[]{:S(2)}) async-start(bf16[16,128,128]{2,1,0:T(8,128)(2,1)} %gather.1), calls=%async_computation.1 | async-start | bytes 1048576 | tf_op jit(solution)/shard_map/all_to_all | solution.py:332
  19.1 0.0 copy-done.7
  19.1 0.0 copy-start.1
  19.1 0.0 copy-start.2
  19.1 0.0 copy-start.5
  19.2 0.5 %copy.14.env = bf16[4,26,4096]{2,1,0:T(8,128)(2,1)S(1)} copy(bf16[4,26,4096]{2,0,1:T(4,128)(2,1)S(1)} %copy-done.7) | data formatting | bytes 1703936 | tf_op args[1]
  19.7 0.3 copy-done.1
  20.0 0.0 copy-done.2
  20.0 0.0 copy-done.5
  20.0 1.3 %left.1 = (bf16[8,64,128]{2,1,0:T(8,128)(2,1)S(1)}, bf16[8,64,128]{2,1,0:T(8,128)(2,1)S(1)}, f32[8,64,64]{2,1,0:T(8,128)S(1)}, s32[1,8]{1,0:T(1,128)S(1)}) custom-call(s32[8]{0:T(128)S(1)} %copy-done.5, s32[1,8]{1,0:T(1,128)S(1)} %bitcast.19, f32[8,2,26]{2,1,0:T(2,128)S(1)} %copy-done.2, bf16[4,26,4096]{2,1,0:T(8,128)(2,1)S(1)} %copy.14.env, ...), custom_call_target="tpu_custom_call" | custom-call | flops 100000000 | bytes 3000000 | tf_op jit(solution)/shard_map/left/pallas_call | solution.py:357
  21.3 10.1 %all-to-all-done.1 = bf16[16,128,128]{2,1,0:T(8,128)(2,1)S(1)} async-done(((bf16[16,128,128]{2,1,0:T(8,128)(2,1)}), bf16[16,128,128]{2,1,0:T(8,128)(2,1)S(1)}, u32[]{:S(2)}, u32[]{:S(2)}) %all-to-all-start.1) | async-done | bytes 524320 | tf_op jit(solution)/shard_map/all_to_all | solution.py:332
  31.4 1.1 %image.1 = (f32[8,64,64]{2,1,0:T(8,128)S(1)}, bf16[8,128,64]{2,1,0:T(8,128)(2,1)S(1)}, f32[16,128]{1,0:T(8,128)S(1)}) custom-call(s32[1,8]{1,0:T(1,128)S(1)} %get-tuple-element.10.slot, bf16[32,64,128]{2,1,0:T(8,128)(2,1)S(1)} %bitcast.13, bf16[8,64,128]{2,1,0:T(8,128)(2,1)S(1)} %get-tuple-element.11.lcomb, bf16[8,64,128]{2,1,0:T(8,128)(2,1)S(1)} %get-tuple-element.12.image, ...), custom_call_target="tpu_custom_call" | custom-call | tf_op jit(solution)/shard_map/image/pallas_call | solution.py:388
  32.5 8.6 %all_to_all.15 = f32[16,1,128]{2,1,0:T(1,128)S(1)} all-to-all(f32[16,1,128]{2,1,0:T(1,128)S(1)} %bitcast.17), channel_id=1, replica_groups={{9,6,0,3,11,2,4,14,1,10,12,15,8,7,13,5},{25,22,16,19,27,18,20,30,17,26,..., dimensions={0} | all-to-all | bytes 16384 | tf_op jit(solution)/shard_map/all_to_all | solution.py:332
  41.1 1.5 %second.1 = (f32[8,4096]{1,0:T(8,128)}, bf16[8,4096]{1,0:T(8,128)(2,1)}, f32[3]{0:T(128)}) custom-call(f32[16,128]{1,0:T(8,128)S(1)} %bitcast.16, f32[8,64,64]{2,1,0:T(8,128)S(1)} %get-tuple-element.15.hpsi, f32[8,64,64]{2,1,0:T(8,128)S(1)} %get-tuple-element.13.wave, bf16[8,128,64]{2,1,0:T(8,128)(2,1)S(1)} %get-tuple-element.16.rsel, ...), custom_call_target="tpu_custom_call" | custom-call | tf_op jit(solution)/shard_map/second/pallas_call | solution.py:408
Async XLA Ops:
  0.6 0.7 %copy-start.6 = (s32[8]{0:T(128)S(1)}, s32[8]{0:T(128)}, u32[]{:S(2)}) copy-start(s32[8]{0:T(128)} %param.14) | copy-start | bytes 100
  0.6 0.7 %copy-start.3 = (s32[8,1]{0,1:T(1,128)S(1)}, s32[8,1]{0,1:T(1,128)}, u32[]{:S(2)}) copy-start(s32[8,1]{0,1:T(1,128)} %param.13) | copy-start | bytes 100
  0.7 0.7 %copy-start.4 = (s32[8,2]{0,1:T(2,128)S(1)}, s32[8,2]{0,1:T(2,128)}, u32[]{:S(2)}) copy-start(s32[8,2]{0,1:T(2,128)} %param.15) | copy-start | bytes 196
  2.1 11.7 %all-to-all-start = ((s32[16,1,4]{2,1,0:T(1,128)}), s32[16,1,4]{2,1,0:T(1,128)S(1)}, u32[]{:S(2)}, u32[]{:S(2)}) async-start(s32[16,1,4]{2,1,0:T(1,128)} %bitcast.10), calls=%async_computation | async-start | bytes 16384 | tf_op jit(solution)/shard_map/all_to_all | solution.py:332
  9.6 1.2 %copy-start = (bf16[4,26,4096]{2,0,1:T(4,128)(2,1)S(1)}, bf16[4,26,4096]{2,0,1:T(4,128)(2,1)}, u32[]{:S(2)}) copy-start(bf16[4,26,4096]{2,0,1:T(4,128)(2,1)} %param.10) | copy-start | bytes 2555908
  14.7 4.4 %copy-start.7 = (bf16[4,26,4096]{2,0,1:T(4,128)(2,1)S(1)}, bf16[4,26,4096]{2,0,1:T(4,128)(2,1)}, u32[]{:S(2)}) copy-start(bf16[4,26,4096]{2,0,1:T(4,128)(2,1)} %param.9) | copy-start | bytes 2555908
  14.7 16.7 %all-to-all-start.1 = ((bf16[16,128,128]{2,1,0:T(8,128)(2,1)}), bf16[16,128,128]{2,1,0:T(8,128)(2,1)S(1)}, u32[]{:S(2)}, u32[]{:S(2)}) async-start(bf16[16,128,128]{2,1,0:T(8,128)(2,1)} %gather.1), calls=%async_computation.1 | async-start | bytes 1048576 | tf_op jit(solution)/shard_map/all_to_all | solution.py:332
  19.1 0.8 %copy-start.1 = (bf16[8,4096]{1,0:T(8,128)(2,1)S(1)}, bf16[8,4096]{1,0:T(8,128)(2,1)}, u32[]{:S(2)}) copy-start(bf16[8,4096]{1,0:T(8,128)(2,1)} %psi.1) | copy-start | bytes 196612
  19.1 0.8 %copy-start.2 = (f32[8,2,26]{2,1,0:T(2,128)S(1)}, f32[8,2,26]{2,1,0:T(2,128)}, u32[]{:S(2)}) copy-start(f32[8,2,26]{2,1,0:T(2,128)} %couple.1) | copy-start | bytes 4996
  19.1 0.8 %copy-start.5 = (s32[8]{0:T(128)S(1)}, s32[8]{0:T(128)}, u32[]{:S(2)}) copy-start(s32[8]{0:T(128)} %sector.1) | copy-start | bytes 100

commit v5 on v4

--- a/solution.py
+++ b/solution.py
@@ -81,15 +81,6 @@
     table[...] = filled[:, : table.shape[1]]
 
 
-def right_kernel(env, out, stage):
-    chans, rsecs, _ = env.shape
-    for w in range(chans):
-        rows = env[w].astype(F32)
-        for t in range(TILES):
-            stage[pl.ds(w * rsecs * TILES + t, rsecs, stride=TILES), :] = rows[:, t * LANES : (t + 1) * LANES]
-    out[...] = stage[...].reshape(out.shape).astype(BF16)
-
-
 def gather_kernel(table, env, out):
     peers = out.shape[0]
     run = run_of(MATRIX_ORDER, peers)
@@ -104,13 +95,41 @@
         each(run or peers, fill)
 
 
-def left_kernel(peers, sector, owner, couple, env, psi, lcomb, image, wave, slot, weights, envs, stage, twice):
+def prepare_kernel(
+    peers, sector_far, owner_far, couple_far, psi_far, left_far, right_far, right, lcomb, image, wave, slot,
+    sector, owner, couple, psi, left_env, right_env, arrived, flat, right_stage, stage, twice,
+):
     blocks, terms, chans = couple.shape
-    lsecs = env.shape[0]
-    wide = envs.shape[0]
-    pitch = wide // lsecs
+    lsecs = left_env.shape[1]
+    rsecs = right_env.shape[1]
+    wide = flat.shape[0]
     rows = blocks * terms
-
+    moves = [
+        pltpu.make_async_copy(source, target, arrived.at[i])
+        for i, (source, target) in enumerate(
+            (
+                (right_far, right_env),
+                (left_far, left_env),
+                (psi_far, psi),
+                (couple_far, couple),
+                (sector_far, sector),
+                (owner_far, owner),
+            )
+        )
+    ]
+    for move in moves:
+        move.start()
+    flat[chans * lsecs :, :] = jnp.zeros((wide - chans * lsecs, B * B), F32)
+    moves[0].wait()
+
+    for w in range(chans):
+        slab = right_env[w].astype(F32)
+        for t in range(TILES):
+            right_stage[pl.ds(w * rsecs * TILES + t, rsecs, stride=TILES), :] = slab[:, t * LANES : (t + 1) * LANES]
+    right[...] = right_stage[...].reshape(right.shape).astype(BF16)
+
+    for move in moves[1:]:
+        move.wait()
     own = owner[...]
     lane = lax.broadcasted_iota(jnp.int32, own.shape, 1)
     rank = jnp.zeros_like(own)
@@ -119,33 +138,39 @@
     place = [(peer, q) for q, peer in enumerate(MATRIX_ORDER)]
     slot[...] = replaced(own, place, run_of(MATRIX_ORDER, peers)) * CAP + rank
 
-    weights[...] = jnp.zeros_like(weights)
-    envs[...] = jnp.zeros_like(envs)
-    for s in range(lsecs):
-        envs[s * pitch : s * pitch + chans, :] = env[s]
-
-    def weigh(k):
-        for j in range(terms):
-            weights[pl.ds(j * blocks + k, 1), 0:chans] = couple[k, j : j + 1]
-
-    each(blocks, weigh)
-
-    def turn(k):
-        for j in range(terms):
-            place = pl.ds(j * blocks + k, 1)
-            weights[place, :] = pltpu.roll(weights[place, :], sector[k] * pitch, 1)
-
-    each(blocks, turn)
-    exact = weights[...]
+    is_low = low_half()
+
+    waves = psi[...].astype(F32)
+    for g in range(blocks // 8):
+        for t in range(TILES):
+            tile = waves[8 * g : 8 * g + 8, t * LANES : (t + 1) * LANES]
+            base = 8 * g * B + 2 * t
+            twice[pl.ds(base, 8, stride=B), :] = jnp.where(is_low, tile, swap(tile))
+            twice[pl.ds(base + 1, 8, stride=B), :] = jnp.where(is_low, swap(tile), tile)
+
+    exact = jnp.concatenate([couple[:, j, :] for j in range(terms)], axis=0)
     high = exact.astype(BF16)
     rest = exact - high.astype(F32)
     middle = rest.astype(BF16)
     low = (rest - middle.astype(F32)).astype(BF16)
-    parts = jnp.concatenate([high, middle, low], axis=0)
-    is_low = low_half()
+    column = lax.broadcasted_iota(jnp.int32, (chans, wide), 1)
+    begin = lax.broadcasted_iota(jnp.int32, (chans, wide), 0) * lsecs
+    spreads = ((column >= begin) & (column < begin + lsecs)).astype(F32).astype(BF16)
+    wider = dot(jnp.concatenate([high, middle, low], axis=0), spreads)
+    row = lax.broadcasted_iota(jnp.int32, (blocks, wide), 0)
+    of_lane = lax.rem(lax.broadcasted_iota(jnp.int32, (blocks, wide), 1), lsecs)
+    own_sector = sector[...]
+    chosen = jnp.zeros((blocks, wide), jnp.int32)
+    for k in range(blocks):
+        chosen = jnp.where(row == k, own_sector[:, k : k + 1], chosen)
+    mask = (chosen == of_lane).astype(F32)
+    parts = (wider * jnp.concatenate([mask] * (3 * terms), axis=0)).astype(BF16)
+
+    for w in range(chans):
+        flat[w * lsecs : (w + 1) * lsecs, :] = left_env[w].astype(F32)
     width = 512
     for n in range(B * B // width):
-        sums = dot(parts, envs[:, n * width : (n + 1) * width])
+        sums = dot(parts, flat[:, n * width : (n + 1) * width].astype(BF16))
         total = sums[:rows] + (sums[rows : 2 * rows] + sums[2 * rows :])
         for g in range(blocks // 8):
             for t in range(width // LANES):
@@ -156,15 +181,6 @@
                 stage[pl.ds(base, 8, stride=B), :] = jnp.where(is_low, first, swap(other))
                 stage[pl.ds(base + 1, 8, stride=B), :] = jnp.where(is_low, swap(first), other)
 
-    def waves(g):
-        held = psi[pl.ds(pl.multiple_of(8 * g, 8), 8), :].astype(F32)
-        for t in range(TILES):
-            tile = held[:, t * LANES : (t + 1) * LANES]
-            base = 8 * g * B + 2 * t
-            twice[pl.ds(base, 8, stride=B), :] = jnp.where(is_low, tile, swap(tile))
-            twice[pl.ds(base + 1, 8, stride=B), :] = jnp.where(is_low, swap(tile), tile)
-
-    each(blocks // 8, waves)
     left_lanes = low_half(B)
 
     def block(k):
@@ -338,42 +354,43 @@
         in_specs=[VMEM] * 3,
         out_specs=VMEM,
         compiler_params=params(4),
+        cost_estimate=cost(0, 0),
         name="request",
     )(owner, right_local.reshape(1, blocks), channel.T)
     wanted = exchange(table.reshape(peers, 1, CAP * terms), TABLE_ORDER).reshape(peers, CAP * terms)
 
-    right = pl.pallas_call(
-        right_kernel,
-        out_shape=of((rsecs * chans, TILES, LANES), BF16),
-        in_specs=[VMEM],
-        out_specs=VMEM,
-        scratch_shapes=[pltpu.VMEM((rsecs * chans * TILES, LANES), F32)],
-        compiler_params=params(8),
-        cost_estimate=cost(10_000_000, 3_000_000),
-        name="right",
-    )(right_env.transpose(1, 0, 2))
-
-    wide = rounded_up(lsecs * rounded_up(chans, 32), LANES)
-    lcomb, image, wave, slot = pl.pallas_call(
-        functools.partial(left_kernel, peers),
+    wide = rounded_up(lsecs * chans, LANES)
+    inputs = (
+        left_sector.reshape(1, blocks),
+        owner,
+        couple,
+        psi,
+        left_env.transpose(1, 0, 2),
+        right_env.transpose(1, 0, 2),
+    )
+    right, lcomb, image, wave, slot = pl.pallas_call(
+        functools.partial(prepare_kernel, peers),
         out_shape=(
+            of((chans * rsecs, TILES, LANES), BF16),
             of((blocks, B, terms * B), BF16),
             of((blocks, B, terms * B), BF16),
             of((blocks, B, B), F32),
             of((1, blocks), jnp.int32),
         ),
-        in_specs=[SMEM, VMEM, VMEM, VMEM, VMEM],
-        out_specs=(VMEM,) * 4,
-        scratch_shapes=[
-            pltpu.VMEM((blocks * terms, wide), F32),
-            pltpu.VMEM((wide, B * B), BF16),
+        in_specs=[pl.BlockSpec(memory_space=pl.ANY)] * len(inputs),
+        out_specs=(VMEM,) * 5,
+        scratch_shapes=[pltpu.VMEM(x.shape, x.dtype) for x in inputs]
+        + [
+            pltpu.SemaphoreType.DMA((len(inputs),)),
+            pltpu.VMEM((wide, B * B), F32),
+            pltpu.VMEM((chans * rsecs * TILES, LANES), F32),
             pltpu.VMEM((blocks * B, LANES), F32),
             pltpu.VMEM((blocks * B, LANES), F32),
         ],
         compiler_params=params(24),
         cost_estimate=cost(100_000_000, 3_000_000),
-        name="left",
-    )(left_sector, owner, couple, left_env, psi)
+        name="prepare",
+    )(*[pltpu.with_memory_space_constraint(x, pltpu.HBM) for x in inputs])
 
     sent = pl.pallas_call(
         gather_kernel,

time: 43 us -> 41.4 us (0.963)
  blocking collectives: 8.57 us -> 24.6 us
  waiting for transfers between devices: 12 us -> 1.02 us
  starting transfers between devices: 12 us -> 7.58 us
  local copies, waits for them, and re-layouts: 2.66 us -> 0.69 us
    all_to_all x1 -> x2, blocking collectives: 8.57 us -> 24.6 us  [exchange(): lax.all_to_all(values, 'sec', split_axis=0, concat_axis=0, axis_index_gro...]
    all_to_all x2 -> x1, waiting for transfers between devices: 12 us -> 1.02 us  [exchange(): lax.all_to_all(values, 'sec', split_axis=0, concat_axis=0, axis_index_gro...]
    all_to_all x2 -> x1, starting transfers between devices: 12 us -> 7.58 us  [exchange(): lax.all_to_all(values, 'sec', split_axis=0, concat_axis=0, axis_index_gro...]
    unnamed x17 -> x6, local copies, waits for them, and re-layouts: 2.66 us -> 0.69 us
    pallas_call x1, Pallas kernels: 0.96 us -> 0.16 us  [per_device(): pl.pallas_call(gather_kernel, out_shape=of((peers, CAP * terms * TILES, L...]
    pallas_call x2 -> x1, Pallas kernels: 2.3 us -> 3.06 us  [per_device(): pl.pallas_call(functools.partial(prepare_kernel, peers), out_shape=(of((c...]
  transfers between devices with their start and end apart: 2 -> 1, of which waited for: 2 -> 1; matrix products, arithmetic and copies ran while one was open for 1% -> 0% of each run, Pallas kernels for 5% -> 7%
where the time goes in v5:
time: 41.4 us; the launch traced here: 41.1 us
  blocking collectives  24.6 us (59%)
  starting transfers between devices  7.58 us (18%)
  Pallas kernels  6.58 us (16%)
  waiting for transfers between devices  1.02 us (2%)
  local copies, waits for them, and re-layouts  0.69 us (2%)
  between operations  0.67 us (2%)
    all_to_all x2, blocking collectives, exchange(): lax.all_to_all(values, 'sec', split_axis=0, concat_axis=0, axis_index_gro...  24.6 us
    all_to_all x1, starting transfers between devices, exchange(): lax.all_to_all(values, 'sec', split_axis=0, concat_axis=0, axis_index_gro...  7.58 us
    pallas_call x1, Pallas kernels, per_device(): pl.pallas_call(functools.partial(prepare_kernel, peers), out_shape=(of((c...  3.06 us
    pallas_call x1, Pallas kernels, per_device(): pl.pallas_call(functools.partial(second_kernel, float(blocks * peers * B...  1.5 us
    pallas_call x1, Pallas kernels, per_device(): pl.pallas_call(image_kernel, out_shape=(of((blocks, B, B), F32), of((bloc...  1.13 us
    all_to_all x1, waiting for transfers between devices, exchange(): lax.all_to_all(values, 'sec', split_axis=0, concat_axis=0, axis_index_gro...  1.02 us
  transfers between devices with their start and end apart: 1, of which 1 were waited for; matrix products, arithmetic and copies ran while one was open for 0% of the time, Pallas kernels for 7%

profile of v5, /device:TPU:0, one launch (start us, length us, event | category | flops | bytes accessed | tf_op | source)
XLA Modules:
  0.0 41.1 jit_solution(5721070957011074750)
XLA Ops:
  0.6 0.0 copy-start.2
  0.6 0.0 copy-start
  0.7 0.0 copy-start.1
  0.7 0.6 %copy-done.2 = s32[8]{0:T(128)S(1)} copy-done((s32[8]{0:T(128)S(1)}, s32[8]{0:T(128)}, u32[]{:S(2)}) %copy-start.2) | copy-done | bytes 56
  1.3 0.0 copy-done
  1.3 0.0 copy-done.1
  1.3 0.7 %request.1 = s32[16,4]{1,0:T(8,128)} custom-call(s32[1,8]{1,0:T(1,128)S(1)} %bitcast.20, s32[1,8]{1,0:T(1,128)S(1)} %bitcast.22, s32[2,8]{1,0:T(2,128)S(1)} %bitcast.21), custom_call_target="tpu_custom_call" | custom-call | tf_op jit(solution)/shard_map/request/pallas_call | solution.py:351
  2.1 7.6 %all-to-all-start = ((s32[16,1,4]{2,1,0:T(1,128)}), s32[16,1,4]{2,1,0:T(1,128)S(1)}, u32[]{:S(2)}, u32[]{:S(2)}) async-start(s32[16,1,4]{2,1,0:T(1,128)} %bitcast.12), calls=%async_computation | async-start | bytes 16384 | tf_op jit(solution)/shard_map/all_to_all | solution.py:348
  9.6 3.1 %prepare.1 = (bf16[104,32,128]{2,1,0:T(8,128)(2,1)S(1)}, bf16[8,64,128]{2,1,0:T(8,128)(2,1)S(1)}, bf16[8,64,128]{2,1,0:T(8,128)(2,1)S(1)}, f32[8,64,64]{2,1,0:T(8,128)S(1)}, s32[1,8]{1,0:T(1,128)S(1)}) custom-call(s32[1,8]{1,0:T(1,128)} %bitcast.25, s32[1,8]{1,0:T(1,128)} %bitcast.19, f32[8,2,26]{2,1,0:T(2,128)} %couple_far.1, bf16[8,4096]{1,0:T(8,128)(2,1)} %psi_far.1, ...), custom_call_target="tpu_custom_call" | custom-call | flops 100000000 | bytes 3000000 | tf_op jit(solution)/shard_map/prepare/pallas_call | solution.py:371
  12.7 1.0 %all-to-all-done = s32[16,1,4]{2,1,0:T(1,128)S(1)} async-done(((s32[16,1,4]{2,1,0:T(1,128)}), s32[16,1,4]{2,1,0:T(1,128)S(1)}, u32[]{:S(2)}, u32[]{:S(2)}) %all-to-all-start) | async-done | bytes 288 | tf_op jit(solution)/shard_map/all_to_all | solution.py:348
  13.7 0.2 gather.1
  13.9 16.0 %all_to_all.15 = bf16[16,128,128]{2,1,0:T(8,128)(2,1)S(1)} all-to-all(bf16[16,128,128]{2,1,0:T(8,128)(2,1)S(1)} %gather.1), channel_id=1, replica_groups={{9,11,5,15,12,8,6,1,10,3,4,14,7,0,13,2},{25,27,21,31,28,24,22,17,26,19,..., dimensions={0} | all-to-all | bytes 1048576 | tf_op jit(solution)/shard_map/all_to_all | solution.py:348
  29.9 1.1 %image.1 = (f32[8,64,64]{2,1,0:T(8,128)S(1)}, bf16[8,128,64]{2,1,0:T(8,128)(2,1)S(1)}, f32[16,128]{1,0:T(8,128)S(1)}) custom-call(s32[1,8]{1,0:T(1,128)S(1)} %get-tuple-element.11.slot, bf16[32,64,128]{2,1,0:T(8,128)(2,1)S(1)} %bitcast.15, bf16[8,64,128]{2,1,0:T(8,128)(2,1)S(1)} %get-tuple-element.13.lcomb, bf16[8,64,128]{2,1,0:T(8,128)(2,1)S(1)} %get-tuple-element.14.image, ...), custom_call_target="tpu_custom_call" | custom-call | tf_op jit(solution)/shard_map/image/pallas_call | solution.py:405
  31.1 8.5 %all_to_all.16 = f32[16,1,128]{2,1,0:T(1,128)S(1)} all-to-all(f32[16,1,128]{2,1,0:T(1,128)S(1)} %bitcast.18), channel_id=1, replica_groups={{9,6,0,3,11,2,4,14,1,10,12,15,8,7,13,5},{25,22,16,19,27,18,20,30,17,26,..., dimensions={0} | all-to-all | bytes 16384 | tf_op jit(solution)/shard_map/all_to_all | solution.py:348
  39.6 1.5 %second.1 = (f32[8,4096]{1,0:T(8,128)}, bf16[8,4096]{1,0:T(8,128)(2,1)}, f32[3]{0:T(128)}) custom-call(f32[16,128]{1,0:T(8,128)S(1)} %bitcast.17, f32[8,64,64]{2,1,0:T(8,128)S(1)} %get-tuple-element.17.hpsi, f32[8,64,64]{2,1,0:T(8,128)S(1)} %get-tuple-element.15.wave, bf16[8,128,64]{2,1,0:T(8,128)(2,1)S(1)} %get-tuple-element.18.rsel, ...), custom_call_target="tpu_custom_call" | custom-call | tf_op jit(solution)/shard_map/second/pallas_call | solution.py:425
Async XLA Ops:
  0.6 0.7 %copy-start.2 = (s32[8]{0:T(128)S(1)}, s32[8]{0:T(128)}, u32[]{:S(2)}) copy-start(s32[8]{0:T(128)} %param.14) | copy-start | bytes 100
  0.6 0.7 %copy-start = (s32[8,1]{0,1:T(1,128)S(1)}, s32[8,1]{0,1:T(1,128)}, u32[]{:S(2)}) copy-start(s32[8,1]{0,1:T(1,128)} %param.13) | copy-start | bytes 100
  0.7 0.7 %copy-start.1 = (s32[8,2]{0,1:T(2,128)S(1)}, s32[8,2]{0,1:T(2,128)}, u32[]{:S(2)}) copy-start(s32[8,2]{0,1:T(2,128)} %param.15) | copy-start | bytes 196
  2.1 11.7 %all-to-all-start = ((s32[16,1,4]{2,1,0:T(1,128)}), s32[16,1,4]{2,1,0:T(1,128)S(1)}, u32[]{:S(2)}, u32[]{:S(2)}) async-start(s32[16,1,4]{2,1,0:T(1,128)} %bitcast.12), calls=%async_computation | async-start | bytes 16384 | tf_op jit(solution)/shard_map/all_to_all | solution.py:348

commit v6 on v5

--- a/solution.py
+++ b/solution.py
@@ -14,9 +14,7 @@
 STATS = 7
 SPACE = 16
 TINY = 1e-30
-TABLE_ORDER = (9, 11, 12, 15, 0, 14, 6, 1, 8, 3, 4, 10, 7, 5, 13, 2)
-MATRIX_ORDER = (9, 11, 5, 15, 12, 8, 6, 1, 10, 3, 4, 14, 7, 0, 13, 2)
-SUM_ORDER = (9, 6, 0, 3, 11, 2, 4, 14, 1, 10, 12, 15, 8, 7, 13, 5)
+ORDER = (11, 2, 14, 6, 9, 7, 13, 10, 8, 5, 4, 12, 1, 15, 0, 3)
 F32 = jnp.float32
 BF16 = jnp.bfloat16
 
@@ -33,16 +31,17 @@
         pl.loop(0, count)(body)
 
 
-def run_of(order, peers):
-    return 0 if peers % len(order) else peers // len(order)
-
-
-def listed(order, peers):
-    run = run_of(order, peers)
-    return [q * run + i for q in order for i in range(run)] if run else list(range(peers))
-
-
-def replaced(values, pairs, run):
+def run_of(peers):
+    return 0 if peers % len(ORDER) else peers // len(ORDER)
+
+
+def listed(peers):
+    run = run_of(peers)
+    return [q * run + i for q in ORDER for i in range(run)] if run else list(range(peers))
+
+
+def replaced(values, pairs, peers):
+    run = run_of(peers)
     if not run:
         return values
     whole = values // run if run > 1 else values
@@ -68,7 +67,7 @@
     terms, blocks = channel.shape
     peers = table.shape[0]
     peer = lax.broadcasted_iota(jnp.int32, (peers, LANES), 0)
-    peer = replaced(peer, enumerate(TABLE_ORDER), run_of(TABLE_ORDER, peers))
+    peer = replaced(peer, enumerate(ORDER), peers)
     lane = lax.broadcasted_iota(jnp.int32, (peers, LANES), 1)
     wanted = channel[...] * rsecs + local[...]
     seen = jnp.zeros((peers, LANES), jnp.int32)
@@ -82,17 +81,12 @@
 
 
 def gather_kernel(table, env, out):
-    peers = out.shape[0]
-    run = run_of(MATRIX_ORDER, peers)
-    starts = [(q * run, TABLE_ORDER.index(peer) * run) for q, peer in enumerate(MATRIX_ORDER)] if run else [(0, 0)]
-    for target, source in starts:
-
-        def fill(p):
-            wanted = table[pl.ds(source + p, 1), :]
-            for i in range(table.shape[1]):
-                out[target + p, i * TILES : (i + 1) * TILES, :] = env[wanted[0, i]]
-
-        each(run or peers, fill)
+    def fill(p):
+        wanted = table[pl.ds(p, 1), :]
+        for i in range(table.shape[1]):
+            out[p, i * TILES : (i + 1) * TILES, :] = env[wanted[0, i]]
+
+    each(out.shape[0], fill)
 
 
 def prepare_kernel(
@@ -126,7 +120,7 @@
         slab = right_env[w].astype(F32)
         for t in range(TILES):
             right_stage[pl.ds(w * rsecs * TILES + t, rsecs, stride=TILES), :] = slab[:, t * LANES : (t + 1) * LANES]
-    right[...] = right_stage[...].reshape(right.shape).astype(BF16)
+    right[...] = right_stage[: chans * rsecs * TILES, :].reshape(right.shape).astype(BF16)
 
     for move in moves[1:]:
         move.wait()
@@ -135,15 +129,14 @@
     rank = jnp.zeros_like(own)
     for k in range(blocks):
         rank = rank + ((own == own[:, k : k + 1]) & (lane > k)).astype(jnp.int32)
-    place = [(peer, q) for q, peer in enumerate(MATRIX_ORDER)]
-    slot[...] = replaced(own, place, run_of(MATRIX_ORDER, peers)) * CAP + rank
+    slot[...] = replaced(own, [(peer, q) for q, peer in enumerate(ORDER)], peers) * CAP + rank
 
     is_low = low_half()
 
-    waves = psi[...].astype(F32)
     for g in range(blocks // 8):
+        waves = psi[g].astype(F32)
         for t in range(TILES):
-            tile = waves[8 * g : 8 * g + 8, t * LANES : (t + 1) * LANES]
+            tile = waves[:, t * LANES : (t + 1) * LANES]
             base = 8 * g * B + 2 * t
             twice[pl.ds(base, 8, stride=B), :] = jnp.where(is_low, tile, swap(tile))
             twice[pl.ds(base + 1, 8, stride=B), :] = jnp.where(is_low, swap(tile), tile)
@@ -343,8 +336,8 @@
     groups = blocks // 8
     of = jax.ShapeDtypeStruct
 
-    def exchange(values, order):
-        members = [listed(order, peers)]
+    def exchange(values):
+        members = [listed(peers)]
         return lax.all_to_all(values, "sec", split_axis=0, concat_axis=0, axis_index_groups=members, tiled=True)
 
     owner = right_owner.T
@@ -357,14 +350,14 @@
         cost_estimate=cost(0, 0),
         name="request",
     )(owner, right_local.reshape(1, blocks), channel.T)
-    wanted = exchange(table.reshape(peers, 1, CAP * terms), TABLE_ORDER).reshape(peers, CAP * terms)
+    wanted = exchange(table.reshape(peers, 1, CAP * terms)).reshape(peers, CAP * terms)
 
     wide = rounded_up(lsecs * chans, LANES)
     inputs = (
         left_sector.reshape(1, blocks),
         owner,
         couple,
-        psi,
+        psi.reshape(groups, 8, B * B),
         left_env.transpose(1, 0, 2),
         right_env.transpose(1, 0, 2),
     )
@@ -383,9 +376,9 @@
         + [
             pltpu.SemaphoreType.DMA((len(inputs),)),
             pltpu.VMEM((wide, B * B), F32),
-            pltpu.VMEM((chans * rsecs * TILES, LANES), F32),
-            pltpu.VMEM((blocks * B, LANES), F32),
-            pltpu.VMEM((blocks * B, LANES), F32),
+            pltpu.VMEM(((chans * rsecs + 1) * TILES, LANES), F32),
+            pltpu.VMEM(((blocks + 1) * B, LANES), F32),
+            pltpu.VMEM(((blocks + 1) * B, LANES), F32),
         ],
         compiler_params=params(24),
         cost_estimate=cost(100_000_000, 3_000_000),
@@ -400,7 +393,7 @@
         compiler_params=params(8),
         name="gather",
     )(wanted, right)
-    received = exchange(sent, MATRIX_ORDER).reshape(slots, terms * TILES, LANES)
+    received = exchange(sent).reshape(slots, terms * TILES, LANES)
 
     hpsi, rsel, stats = pl.pallas_call(
         image_kernel,
@@ -412,15 +405,15 @@
         in_specs=[VMEM] * 5,
         out_specs=(VMEM, VMEM, VMEM),
         scratch_shapes=[
-            pltpu.VMEM((blocks * terms * B, LANES), F32),
+            pltpu.VMEM(((blocks * terms + 1) * B, LANES), F32),
             pltpu.VMEM((blocks, B, B), F32),
             pltpu.VMEM((blocks, terms * B, B), BF16),
-            pltpu.VMEM((STATS, blocks * 8, B), F32),
+            pltpu.VMEM((STATS, (blocks + 1) * 8, B), F32),
         ],
         compiler_params=params(24),
         name="image",
     )(slot, received, lcomb, image, wave)
-    stats = exchange(stats.reshape(peers, groups, LANES), SUM_ORDER).reshape(peers * groups, LANES)
+    stats = exchange(stats.reshape(peers, groups, LANES)).reshape(peers * groups, LANES)
 
     second, direction, projected = pl.pallas_call(
         functools.partial(second_kernel, float(blocks * peers * B * B)),
@@ -428,8 +421,8 @@
         in_specs=[VMEM] * 5,
         out_specs=(VMEM, VMEM, SMEM),
         scratch_shapes=[
-            pltpu.VMEM((blocks * B, LANES), F32),
-            pltpu.VMEM((blocks * B, LANES), F32),
+            pltpu.VMEM(((blocks + 1) * B, LANES), F32),
+            pltpu.VMEM(((blocks + 1) * B, LANES), F32),
             pltpu.VMEM((blocks, terms * B, B), BF16),
             pltpu.VMEM((blocks, B, B), BF16),
         ],

time: 41.4 us -> 41.1 us (level)
  waiting for transfers between devices: 1.02 us -> 0.07 us
    all_to_all x1, waiting for transfers between devices: 1.02 us -> 0.07 us  [exchange(): lax.all_to_all(values, 'sec', split_axis=0, concat_axis=0, axis_index_gro...]
  transfers between devices with their start and end apart: 1 -> 1, of which waited for: 1 -> 1; matrix products, arithmetic and copies ran while one was open for 0% -> 0% of each run, Pallas kernels for 7% -> 8%
where the time goes in v6:
time: 41.1 us; the launch traced here: 40.8 us
  blocking collectives  25 us (61%)
  starting transfers between devices  7.8 us (19%)
  Pallas kernels  6.58 us (16%)
  local copies, waits for them, and re-layouts  0.69 us (2%)
  between operations  0.67 us (2%)
    all_to_all x2, blocking collectives, exchange(): lax.all_to_all(values, 'sec', split_axis=0, concat_axis=0, axis_index_gro...  25 us
    all_to_all x1, starting transfers between devices, exchange(): lax.all_to_all(values, 'sec', split_axis=0, concat_axis=0, axis_index_gro...  7.8 us
    pallas_call x1, Pallas kernels, per_device(): pl.pallas_call(functools.partial(prepare_kernel, peers), out_shape=(of((c...  3.06 us
    pallas_call x1, Pallas kernels, per_device(): pl.pallas_call(functools.partial(second_kernel, float(blocks * peers * B...  1.51 us
    pallas_call x1, Pallas kernels, per_device(): pl.pallas_call(image_kernel, out_shape=(of((blocks, B, B), F32), of((bloc...  1.13 us
  transfers between devices with their start and end apart: 1, of which 1 were waited for; matrix products, arithmetic and copies ran while one was open for 0% of the time, Pallas kernels for 8%

profile of v6, /device:TPU:0, one launch (start us, length us, event | category | flops | bytes accessed | tf_op | source)
XLA Modules:
  0.0 40.8 jit_solution(17739063190492370345)
XLA Ops:
  0.6 0.0 copy-start.2
  0.6 0.0 copy-start
  0.7 0.0 copy-start.1
  0.7 0.6 %copy-done.2 = s32[8]{0:T(128)S(1)} copy-done((s32[8]{0:T(128)S(1)}, s32[8]{0:T(128)}, u32[]{:S(2)}) %copy-start.2) | copy-done | bytes 56
  1.3 0.0 copy-done
  1.3 0.0 copy-done.1
  1.3 0.7 %request.1 = s32[16,4]{1,0:T(8,128)} custom-call(s32[1,8]{1,0:T(1,128)S(1)} %bitcast.21, s32[1,8]{1,0:T(1,128)S(1)} %bitcast.23, s32[2,8]{1,0:T(2,128)S(1)} %bitcast.22), custom_call_target="tpu_custom_call" | custom-call | tf_op jit(solution)/shard_map/request/pallas_call | solution.py:344
  2.1 7.8 %all-to-all-start = ((s32[16,1,4]{2,1,0:T(1,128)}), s32[16,1,4]{2,1,0:T(1,128)S(1)}, u32[]{:S(2)}, u32[]{:S(2)}) async-start(s32[16,1,4]{2,1,0:T(1,128)} %bitcast.13), calls=%async_computation | async-start | bytes 16384 | tf_op jit(solution)/shard_map/all_to_all | solution.py:341
  9.9 3.1 %prepare.1 = (bf16[104,32,128]{2,1,0:T(8,128)(2,1)S(1)}, bf16[8,64,128]{2,1,0:T(8,128)(2,1)S(1)}, bf16[8,64,128]{2,1,0:T(8,128)(2,1)S(1)}, f32[8,64,64]{2,1,0:T(8,128)S(1)}, s32[1,8]{1,0:T(1,128)S(1)}) custom-call(s32[1,8]{1,0:T(1,128)} %bitcast.27, s32[1,8]{1,0:T(1,128)} %bitcast.20, f32[8,2,26]{2,1,0:T(2,128)} %couple_far.1, bf16[1,8,4096]{2,1,0:T(8,128)(2,1)} %bitcast.26, ...), custom_call_target="tpu_custom_call" | custom-call | flops 100000000 | bytes 3000000 | tf_op jit(solution)/shard_map/prepare/pallas_call | solution.py:364
  12.9 0.1 all-to-all-done
  13.0 0.2 gather.1
  13.2 17.0 %all_to_all.15 = bf16[16,128,128]{2,1,0:T(8,128)(2,1)S(1)} all-to-all(bf16[16,128,128]{2,1,0:T(8,128)(2,1)S(1)} %gather.1), channel_id=1, replica_groups={{11,2,14,6,9,7,13,10,8,5,4,12,1,15,0,3},{27,18,30,22,25,23,29,26,24,21,..., dimensions={0} | all-to-all | bytes 1048576 | tf_op jit(solution)/shard_map/all_to_all | solution.py:341
  30.2 1.1 %image.1 = (f32[8,64,64]{2,1,0:T(8,128)S(1)}, bf16[8,128,64]{2,1,0:T(8,128)(2,1)S(1)}, f32[16,128]{1,0:T(8,128)S(1)}) custom-call(s32[1,8]{1,0:T(1,128)S(1)} %get-tuple-element.11.slot, bf16[32,64,128]{2,1,0:T(8,128)(2,1)S(1)} %bitcast.16, bf16[8,64,128]{2,1,0:T(8,128)(2,1)S(1)} %get-tuple-element.13.lcomb, bf16[8,64,128]{2,1,0:T(8,128)(2,1)S(1)} %get-tuple-element.14.image, ...), custom_call_target="tpu_custom_call" | custom-call | tf_op jit(solution)/shard_map/image/pallas_call | solution.py:398
  31.3 7.9 %all_to_all.16 = f32[16,1,128]{2,1,0:T(1,128)S(1)} all-to-all(f32[16,1,128]{2,1,0:T(1,128)S(1)} %bitcast.19), channel_id=1, replica_groups={{11,2,14,6,9,7,13,10,8,5,4,12,1,15,0,3},{27,18,30,22,25,23,29,26,24,21,..., dimensions={0} | all-to-all | bytes 16384 | tf_op jit(solution)/shard_map/all_to_all | solution.py:341
  39.3 1.5 %second.1 = (f32[8,4096]{1,0:T(8,128)}, bf16[8,4096]{1,0:T(8,128)(2,1)}, f32[3]{0:T(128)}) custom-call(f32[16,128]{1,0:T(8,128)S(1)} %bitcast.18, f32[8,64,64]{2,1,0:T(8,128)S(1)} %get-tuple-element.17.hpsi, f32[8,64,64]{2,1,0:T(8,128)S(1)} %get-tuple-element.15.wave, bf16[8,128,64]{2,1,0:T(8,128)(2,1)S(1)} %get-tuple-element.18.rsel, ...), custom_call_target="tpu_custom_call" | custom-call | tf_op jit(solution)/shard_map/second/pallas_call | solution.py:418
Async XLA Ops:
  0.6 0.7 %copy-start.2 = (s32[8]{0:T(128)S(1)}, s32[8]{0:T(128)}, u32[]{:S(2)}) copy-start(s32[8]{0:T(128)} %param.14) | copy-start | bytes 100
  0.6 0.7 %copy-start = (s32[8,1]{0,1:T(1,128)S(1)}, s32[8,1]{0,1:T(1,128)}, u32[]{:S(2)}) copy-start(s32[8,1]{0,1:T(1,128)} %param.13) | copy-start | bytes 100
  0.7 0.7 %copy-start.1 = (s32[8,2]{0,1:T(2,128)S(1)}, s32[8,2]{0,1:T(2,128)}, u32[]{:S(2)}) copy-start(s32[8,2]{0,1:T(2,128)} %param.15) | copy-start | bytes 196
  2.1 10.9 %all-to-all-start = ((s32[16,1,4]{2,1,0:T(1,128)}), s32[16,1,4]{2,1,0:T(1,128)S(1)}, u32[]{:S(2)}, u32[]{:S(2)}) async-start(s32[16,1,4]{2,1,0:T(1,128)} %bitcast.13), calls=%async_computation | async-start | bytes 16384 | tf_op jit(solution)/shard_map/all_to_all | solution.py:341

commit v7 on v6

--- a/solution.py
+++ b/solution.py
@@ -11,7 +11,7 @@
 CAP = 2
 LANES = 128
 TILES = B * B // LANES
-STATS = 7
+STATS = 5
 SPACE = 16
 TINY = 1e-30
 ORDER = (11, 2, 14, 6, 9, 7, 13, 10, 8, 5, 4, 12, 1, 15, 0, 3)
@@ -53,6 +53,10 @@
 
 def dot(a, b):
     return jnp.dot(a, b, preferred_element_type=F32)
+
+
+def summed(values):
+    return jnp.sum(jnp.sum(values, axis=0, keepdims=True), axis=1, keepdims=True)
 
 
 def low_half(rows=8):
@@ -90,7 +94,7 @@
 
 
 def prepare_kernel(
-    peers, sector_far, owner_far, couple_far, psi_far, left_far, right_far, right, lcomb, image, wave, slot,
+    peers, sector_far, owner_far, couple_far, psi_far, left_far, right_far, right, lcomb, image, wave, norm, slot,
     sector, owner, couple, psi, left_env, right_env, arrived, flat, right_stage, stage, twice,
 ):
     blocks, terms, chans = couple.shape
@@ -137,9 +141,9 @@
         waves = psi[g].astype(F32)
         for t in range(TILES):
             tile = waves[:, t * LANES : (t + 1) * LANES]
-            base = 8 * g * B + 2 * t
+            base = 8 * g * B + t
             twice[pl.ds(base, 8, stride=B), :] = jnp.where(is_low, tile, swap(tile))
-            twice[pl.ds(base + 1, 8, stride=B), :] = jnp.where(is_low, swap(tile), tile)
+            twice[pl.ds(base + TILES, 8, stride=B), :] = jnp.where(is_low, swap(tile), tile)
 
     exact = jnp.concatenate([couple[:, j, :] for j in range(terms)], axis=0)
     high = exact.astype(BF16)
@@ -170,18 +174,23 @@
                 lanes = slice(t * LANES, (t + 1) * LANES)
                 first = total[8 * g : 8 * g + 8, lanes]
                 other = total[blocks + 8 * g : blocks + 8 * g + 8, lanes]
-                base = 8 * g * B + 2 * (n * (width // LANES) + t)
+                base = 8 * g * B + n * (width // LANES) + t
                 stage[pl.ds(base, 8, stride=B), :] = jnp.where(is_low, first, swap(other))
-                stage[pl.ds(base + 1, 8, stride=B), :] = jnp.where(is_low, swap(first), other)
+                stage[pl.ds(base + TILES, 8, stride=B), :] = jnp.where(is_low, swap(first), other)
 
     left_lanes = low_half(B)
+    column = lax.broadcasted_iota(jnp.int32, (LANES, LANES), 0)
+    within = column & (B - 1)
+    moved = column - within + (within & 1) * TILES + (within >> 1)
+    order = (lax.broadcasted_iota(jnp.int32, (LANES, LANES), 1) == moved).astype(F32).astype(BF16)
 
     def block(k):
         place = pl.ds(pl.multiple_of(k * B, B), B)
-        left = stage[place, :].astype(BF16)
+        left = dot(stage[place, :].astype(BF16), order).astype(BF16)
         base = twice[place, :]
         lcomb[k] = left
-        wave[k] = base[:, :B]
+        wave[k] = base
+        norm[pl.ds(k, 1), :] = summed(base[:, :B] * base[:, :B])
         both = jnp.concatenate([jnp.where(left_lanes, base, 0.0), jnp.where(left_lanes, 0.0, base)], axis=0)
         image[k] = dot(left, both.astype(BF16)).astype(BF16)
 
@@ -189,21 +198,27 @@
 
 
 def fold(values):
-    return jnp.sum(values.reshape(B // 8, 8, B), axis=0)
-
-
-def image_kernel(slot, received, lcomb, image, wave, hpsi, rsel, stats, stage, resid, zed, part):
+    return jnp.sum(values[:, :B].reshape(B // 8, 8, B), axis=0)
+
+
+def packed_rows(values):
+    return jnp.where(low_half(TILES), values[:TILES], values[TILES:])
+
+
+def image_kernel(slot, norm, received, lcomb, image, wave, hpsi, rsel, stats, stage, resid, zed, part):
     blocks = lcomb.shape[0]
     groups = blocks // 8
     places = slot[...]
+    is_low = low_half(B)
 
     for k in range(blocks):
         raw = received[places[0, k]].astype(F32)
-        stage[pl.ds(k * 2 * B, B, stride=2), :] = raw
-        stage[pl.ds(k * 2 * B + 1, B, stride=2), :] = swap(raw)
+        turned = swap(raw)
+        stage[pl.ds(k * 2 * B, B, stride=2), :] = jnp.where(is_low, raw, turned)
+        stage[pl.ds(k * 2 * B + 1, B, stride=2), :] = jnp.where(is_low, turned, raw)
 
     def unfold(k):
-        rsel[k] = stage[pl.ds(pl.multiple_of(k * 2 * B, 2 * B), 2 * B), 0:B].astype(BF16)
+        rsel[k] = stage[pl.ds(pl.multiple_of(k * 2 * B, 2 * B), 2 * B), :].astype(BF16)
 
     each(blocks, unfold)
 
@@ -218,38 +233,34 @@
 
     def apply(k):
         h = dot(image[k], rsel[k])
-        base = wave[k]
         hpsi[k] = h
-        keep(0, k, base * base)
-        keep(1, k, base * h)
+        keep(0, k, wave[k] * h)
 
     each(blocks, apply)
 
     def group(g):
-        norm, cross = of_group(0, g), of_group(1, g)
-        theta = cross / jnp.maximum(norm, TINY)
+        own_norm, cross = norm[pl.ds(g * 8, 8), :], of_group(0, g)
+        theta = cross / jnp.maximum(own_norm, TINY)
 
         for i in range(8):
             k = g * 8 + i
             h, base = hpsi[k], wave[k]
             rest = h - theta[i : i + 1, :] * base
             resid[k] = rest
-            step = rest.astype(BF16)
+            step = rest[:, :B].astype(BF16)
             zed[k, 0:B] = dot(step, rsel[k, 0:B]).astype(BF16)
             zed[k, B : 2 * B] = dot(step, rsel[k, B : 2 * B]).astype(BF16)
-            keep(2, k, rest * rest)
-            keep(3, k, rest * base)
-            keep(4, k, rest * h)
+            keep(1, k, rest * rest)
 
         for i in range(8):
             k = g * 8 + i
             applied = dot(lcomb[k], zed[k])
-            keep(5, k, resid[k] * applied)
-            keep(6, k, wave[k] * applied)
+            keep(2, k, resid[k] * applied)
+            keep(3, k, wave[k] * applied)
 
         lane = lax.broadcasted_iota(jnp.int32, (8, LANES), 1)
         packed = jnp.zeros((8, LANES), F32)
-        for i, value in enumerate([norm, cross] + [of_group(i, g) for i in range(2, STATS)]):
+        for i, value in enumerate([own_norm, cross] + [of_group(i, g) for i in range(1, STATS - 1)]):
             packed = jnp.where(lane == i, value, packed)
         spread = pltpu.roll(packed, 0, 1, stride=SPACE, stride_axis=0)
         row = jnp.sum(spread, axis=0, keepdims=True)
@@ -265,25 +276,27 @@
     blocks = lcomb.shape[0]
     held = stats[...]
     here = lax.broadcasted_iota(jnp.int32, held.shape, 1) % SPACE == 0
-    norm, cross, square, mixed, image, applied, crossed = (
+    norm, cross, square, applied, crossed = (
         jnp.where(here, pltpu.roll(held, (LANES - i) % LANES, 1) if i else held, 0.0) for i in range(STATS)
     )
 
-    def total(values):
-        return jnp.sum(jnp.sum(values, axis=0, keepdims=True), axis=1, keepdims=True)
-
-    theta = total(cross) / total(norm)
-    shift = theta - cross / jnp.maximum(norm, TINY)
-    rr = total(square - 2.0 * shift * mixed + shift * shift * norm)
-    along = total(applied - shift * (image + crossed) + shift * shift * cross)
+    theta = summed(cross) / summed(norm)
+    own = cross / jnp.maximum(norm, TINY)
+    mixed = cross - own * norm
+    image = square + own * mixed
+    shift = theta - own
+    rr = summed(square - 2.0 * shift * mixed + shift * shift * norm)
+    along = summed(applied - shift * (image + crossed) + shift * shift * cross)
     spread = rr / count
     scale = 1.0 / jnp.sqrt(spread + 1e-06)
 
+    def rows_of(k):
+        return pl.ds(k // 8 * (8 * TILES) + k % 8, TILES, stride=8)
+
     def move(k):
-        place = pl.ds(pl.multiple_of(k * B, B), B)
         step = ((hpsi[k] - theta * wave[k]) * scale).astype(BF16)
-        narrow[k] = step
-        steps[place, 0:B] = step.astype(F32)
+        narrow[k] = step[:, :B]
+        steps[rows_of(k), :] = packed_rows(step.astype(F32))
 
     each(blocks, move)
 
@@ -294,19 +307,16 @@
     each(blocks, apply)
 
     def close(k):
-        stage[pl.ds(pl.multiple_of(k * B, B), B), 0:B] = dot(lcomb[k], zed[k])
+        stage[rows_of(k), :] = packed_rows(dot(lcomb[k], zed[k]))
 
     each(blocks, close)
-    is_low = low_half()
 
     def rows(g):
         place = pl.ds(pl.multiple_of(8 * g, 8), 8)
         for source, target in ((steps, direction), (stage, second)):
             for t in range(TILES):
-                base = 8 * g * B + 2 * t
-                even = source[pl.ds(base, 8, stride=B), :]
-                odd = source[pl.ds(base + 1, 8, stride=B), :]
-                target[place, t * LANES : (t + 1) * LANES] = jnp.where(is_low, even, swap(odd)).astype(target.dtype)
+                tile = source[pl.ds(pl.multiple_of((g * TILES + t) * 8, 8), 8), :]
+                target[place, t * LANES : (t + 1) * LANES] = tile.astype(target.dtype)
 
     each(blocks // 8, rows)
     projected[0] = theta[0, 0]
@@ -361,17 +371,18 @@
         left_env.transpose(1, 0, 2),
         right_env.transpose(1, 0, 2),
     )
-    right, lcomb, image, wave, slot = pl.pallas_call(
+    right, lcomb, image, wave, norm, slot = pl.pallas_call(
         functools.partial(prepare_kernel, peers),
         out_shape=(
             of((chans * rsecs, TILES, LANES), BF16),
             of((blocks, B, terms * B), BF16),
             of((blocks, B, terms * B), BF16),
-            of((blocks, B, B), F32),
+            of((blocks, B, LANES), F32),
+            of((blocks, 1), F32),
             of((1, blocks), jnp.int32),
         ),
         in_specs=[pl.BlockSpec(memory_space=pl.ANY)] * len(inputs),
-        out_specs=(VMEM,) * 5,
+        out_specs=(VMEM,) * 6,
         scratch_shapes=[pltpu.VMEM(x.shape, x.dtype) for x in inputs]
         + [
             pltpu.SemaphoreType.DMA((len(inputs),)),
@@ -398,21 +409,21 @@
     hpsi, rsel, stats = pl.pallas_call(
         image_kernel,
         out_shape=(
-            of((blocks, B, B), F32),
-            of((blocks, terms * B, B), BF16),
+            of((blocks, B, LANES), F32),
+            of((blocks, terms * B, LANES), BF16),
             of((peers * groups, LANES), F32),
         ),
-        in_specs=[VMEM] * 5,
+        in_specs=[VMEM] * 6,
         out_specs=(VMEM, VMEM, VMEM),
         scratch_shapes=[
             pltpu.VMEM(((blocks * terms + 1) * B, LANES), F32),
-            pltpu.VMEM((blocks, B, B), F32),
-            pltpu.VMEM((blocks, terms * B, B), BF16),
-            pltpu.VMEM((STATS, (blocks + 1) * 8, B), F32),
+            pltpu.VMEM((blocks, B, LANES), F32),
+            pltpu.VMEM((blocks, terms * B, LANES), BF16),
+            pltpu.VMEM((STATS - 1, (blocks + 1) * 8, B), F32),
         ],
         compiler_params=params(24),
         name="image",
-    )(slot, received, lcomb, image, wave)
+    )(slot, norm, received, lcomb, image, wave)
     stats = exchange(stats.reshape(peers, groups, LANES)).reshape(peers * groups, LANES)
 
     second, direction, projected = pl.pallas_call(
@@ -421,9 +432,9 @@
         in_specs=[VMEM] * 5,
         out_specs=(VMEM, VMEM, SMEM),
         scratch_shapes=[
-            pltpu.VMEM(((blocks + 1) * B, LANES), F32),
-            pltpu.VMEM(((blocks + 1) * B, LANES), F32),
-            pltpu.VMEM((blocks, terms * B, B), BF16),
+            pltpu.VMEM((blocks * TILES + 8, LANES), F32),
+            pltpu.VMEM((blocks * TILES + 8, LANES), F32),
+            pltpu.VMEM((blocks, terms * B, LANES), BF16),
             pltpu.VMEM((blocks, B, B), BF16),
         ],
         compiler_params=params(24),

time: 41.1 us -> 41 us (level)
  transfers between devices with their start and end apart: 1 -> 1, of which waited for: 1 -> 0; matrix products, arithmetic and copies ran while one was open for 0% -> 0% of each run, Pallas kernels for 8% -> 8%
where the time goes in v7:
time: 41 us; the launch traced here: 40.8 us
  blocking collectives  25 us (61%)
  starting transfers between devices  7.8 us (19%)
  Pallas kernels  6.63 us (16%)
  local copies, waits for them, and re-layouts  0.69 us (2%)
  between operations  0.68 us (2%)
    all_to_all x2, blocking collectives, exchange(): lax.all_to_all(values, 'sec', split_axis=0, concat_axis=0, axis_index_gro...  25 us
    all_to_all x1, starting transfers between devices, exchange(): lax.all_to_all(values, 'sec', split_axis=0, concat_axis=0, axis_index_gro...  7.8 us
    pallas_call x1, Pallas kernels, per_device(): pl.pallas_call(functools.partial(prepare_kernel, peers), out_shape=(of((c...  3.33 us
    pallas_call x1, Pallas kernels, per_device(): pl.pallas_call(functools.partial(second_kernel, float(blocks * peers * B...  1.31 us
    pallas_call x1, Pallas kernels, per_device(): pl.pallas_call(image_kernel, out_shape=(of((blocks, B, LANES), F32), of((...  1.1 us
  transfers between devices with their start and end apart: 1, of which 0 were waited for; matrix products, arithmetic and copies ran while one was open for 0% of the time, Pallas kernels for 8%

profile of v7, /device:TPU:0, one launch (start us, length us, event | category | flops | bytes accessed | tf_op | source)
XLA Modules:
  0.0 40.8 jit_solution(15822140642030028740)
XLA Ops:
  0.6 0.0 copy-start.2
  0.6 0.0 copy-start
  0.7 0.0 copy-start.1
  0.7 0.6 %copy-done.2 = s32[8]{0:T(128)S(1)} copy-done((s32[8]{0:T(128)S(1)}, s32[8]{0:T(128)}, u32[]{:S(2)}) %copy-start.2) | copy-done | bytes 56
  1.3 0.0 copy-done
  1.3 0.0 copy-done.1
  1.3 0.7 %request.1 = s32[16,4]{1,0:T(8,128)} custom-call(s32[1,8]{1,0:T(1,128)S(1)} %bitcast.21, s32[1,8]{1,0:T(1,128)S(1)} %bitcast.23, s32[2,8]{1,0:T(2,128)S(1)} %bitcast.22), custom_call_target="tpu_custom_call" | custom-call | tf_op jit(solution)/shard_map/request/pallas_call | solution.py:354
  2.1 7.8 %all-to-all-start = ((s32[16,1,4]{2,1,0:T(1,128)}), s32[16,1,4]{2,1,0:T(1,128)S(1)}, u32[]{:S(2)}, u32[]{:S(2)}) async-start(s32[16,1,4]{2,1,0:T(1,128)} %bitcast.13), calls=%async_computation | async-start | bytes 16384 | tf_op jit(solution)/shard_map/all_to_all | solution.py:351
  9.9 3.3 %prepare.1 = (bf16[104,32,128]{2,1,0:T(8,128)(2,1)S(1)}, bf16[8,64,128]{2,1,0:T(8,128)(2,1)S(1)}, bf16[8,64,128]{2,1,0:T(8,128)(2,1)S(1)}, f32[8,64,128]{2,1,0:T...) custom-call(s32[1,8]{1,0:T(1,128)} %bitcast.27, s32[1,8]{1,0:T(1,128)} %bitcast.20, f32[8,2,26]{2,1,0:T(2,128)} %couple_far.1, ...), custom_call_target="tpu_custom_call" | custom-call | flops 100000000 | bytes 3000000 | tf_op jit(solution)/shard_map/prepare/pallas_call | solution.py:374
  13.2 0.0 all-to-all-done
  13.2 0.2 gather.1
  13.4 17.0 %all_to_all.15 = bf16[16,128,128]{2,1,0:T(8,128)(2,1)S(1)} all-to-all(bf16[16,128,128]{2,1,0:T(8,128)(2,1)S(1)} %gather.1), channel_id=1, replica_groups={{11,2,14,6,9,7,13,10,8,5,4,12,1,15,0,3},{27,18,30,22,25,23,29,26,24,21,..., dimensions={0} | all-to-all | bytes 1048576 | tf_op jit(solution)/shard_map/all_to_all | solution.py:351
  30.4 1.1 %image.1 = (f32[8,64,128]{2,1,0:T(8,128)S(1)}, bf16[8,128,128]{2,1,0:T(8,128)(2,1)S(1)}, f32[16,128]{1,0:T(8,128)S(1)}) custom-call(s32[1,8]{1,0:T(1,128)S(1)} %get-tuple-element.12.slot, f32[8,1]{1,0:T(8,128)S(1)} %get-tuple-element.13.norm, bf16[32,64,128]{2,1,0:T(8,128)(2,1)S(1)} %bitcast.16, bf16[8,64,128]{2,1,0:T(8,128)(2,1)S(1)} %get-tuple-element.15.lcomb, ...), custom_call_target="tpu_custom_call" | custom-call | tf_op jit(solution)/shard_map/image/pallas_call | solution.py:409
  31.5 8.0 %all_to_all.16 = f32[16,1,128]{2,1,0:T(1,128)S(1)} all-to-all(f32[16,1,128]{2,1,0:T(1,128)S(1)} %bitcast.19), channel_id=1, replica_groups={{11,2,14,6,9,7,13,10,8,5,4,12,1,15,0,3},{27,18,30,22,25,23,29,26,24,21,..., dimensions={0} | all-to-all | bytes 16384 | tf_op jit(solution)/shard_map/all_to_all | solution.py:351
  39.5 1.3 %second.1 = (f32[8,4096]{1,0:T(8,128)}, bf16[8,4096]{1,0:T(8,128)(2,1)}, f32[3]{0:T(128)}) custom-call(f32[16,128]{1,0:T(8,128)S(1)} %bitcast.18, f32[8,64,128]{2,1,0:T(8,128)S(1)} %get-tuple-element.19.hpsi, f32[8,64,128]{2,1,0:T(8,128)S(1)} %get-tuple-element.17.wave, bf16[8,128,128]{2,1,0:T(8,128)(2,1)S(1)} %get-tuple-element.20.rsel, ...), custom_call_target="tpu_custom_call" | custom-call | tf_op jit(solution)/shard_map/second/pallas_call | solution.py:429
Async XLA Ops:
  0.6 0.7 %copy-start.2 = (s32[8]{0:T(128)S(1)}, s32[8]{0:T(128)}, u32[]{:S(2)}) copy-start(s32[8]{0:T(128)} %param.14) | copy-start | bytes 100
  0.6 0.7 %copy-start = (s32[8,1]{0,1:T(1,128)S(1)}, s32[8,1]{0,1:T(1,128)}, u32[]{:S(2)}) copy-start(s32[8,1]{0,1:T(1,128)} %param.13) | copy-start | bytes 100
  0.7 0.7 %copy-start.1 = (s32[8,2]{0,1:T(2,128)S(1)}, s32[8,2]{0,1:T(2,128)}, u32[]{:S(2)}) copy-start(s32[8,2]{0,1:T(2,128)} %param.15) | copy-start | bytes 196
  2.1 11.1 %all-to-all-start = ((s32[16,1,4]{2,1,0:T(1,128)}), s32[16,1,4]{2,1,0:T(1,128)S(1)}, u32[]{:S(2)}, u32[]{:S(2)}) async-start(s32[16,1,4]{2,1,0:T(1,128)} %bitcast.13), calls=%async_computation | async-start | bytes 16384 | tf_op jit(solution)/shard_map/all_to_all | solution.py:351

commit v8 on v7

--- a/solution.py
+++ b/solution.py
@@ -14,7 +14,7 @@
 STATS = 5
 SPACE = 16
 TINY = 1e-30
-ORDER = (11, 2, 14, 6, 9, 7, 13, 10, 8, 5, 4, 12, 1, 15, 0, 3)
+ORDER = (11, 13, 15, 1, 2, 3, 7, 14, 6, 9, 5, 12, 8, 4, 10, 0)
 F32 = jnp.float32
 BF16 = jnp.bfloat16
 

time: 41 us -> 41 us (level)
  no operation moved by 1% of the time
where the time goes in v8:
time: 41 us; the launch traced here: 40.7 us
  blocking collectives  24.9 us (61%)
  starting transfers between devices  7.79 us (19%)
  Pallas kernels  6.63 us (16%)
  local copies, waits for them, and re-layouts  0.69 us (2%)
  between operations  0.68 us (2%)
    all_to_all x2, blocking collectives, exchange(): lax.all_to_all(values, 'sec', split_axis=0, concat_axis=0, axis_index_gro...  24.9 us
    all_to_all x1, starting transfers between devices, exchange(): lax.all_to_all(values, 'sec', split_axis=0, concat_axis=0, axis_index_gro...  7.79 us
    pallas_call x1, Pallas kernels, per_device(): pl.pallas_call(functools.partial(prepare_kernel, peers), out_shape=(of((c...  3.33 us
    pallas_call x1, Pallas kernels, per_device(): pl.pallas_call(functools.partial(second_kernel, float(blocks * peers * B...  1.31 us
    pallas_call x1, Pallas kernels, per_device(): pl.pallas_call(image_kernel, out_shape=(of((blocks, B, LANES), F32), of((...  1.11 us
  transfers between devices with their start and end apart: 1, of which 0 were waited for; matrix products, arithmetic and copies ran while one was open for 0% of the time, Pallas kernels for 8%

profile of v8, /device:TPU:0, one launch (start us, length us, event | category | flops | bytes accessed | tf_op | source)
XLA Modules:
  0.0 40.7 jit_solution(7441455377064503857)
XLA Ops:
  0.6 0.0 copy-start.2
  0.6 0.0 copy-start
  0.7 0.0 copy-start.1
  0.7 0.6 %copy-done.2 = s32[8]{0:T(128)S(1)} copy-done((s32[8]{0:T(128)S(1)}, s32[8]{0:T(128)}, u32[]{:S(2)}) %copy-start.2) | copy-done | bytes 56
  1.3 0.0 copy-done
  1.3 0.0 copy-done.1
  1.3 0.7 %request.1 = s32[16,4]{1,0:T(8,128)} custom-call(s32[1,8]{1,0:T(1,128)S(1)} %bitcast.21, s32[1,8]{1,0:T(1,128)S(1)} %bitcast.23, s32[2,8]{1,0:T(2,128)S(1)} %bitcast.22), custom_call_target="tpu_custom_call" | custom-call | tf_op jit(solution)/shard_map/request/pallas_call | solution.py:354
  2.1 7.8 %all-to-all-start = ((s32[16,1,4]{2,1,0:T(1,128)}), s32[16,1,4]{2,1,0:T(1,128)S(1)}, u32[]{:S(2)}, u32[]{:S(2)}) async-start(s32[16,1,4]{2,1,0:T(1,128)} %bitcast.13), calls=%async_computation | async-start | bytes 16384 | tf_op jit(solution)/shard_map/all_to_all | solution.py:351
  9.8 3.3 %prepare.1 = (bf16[104,32,128]{2,1,0:T(8,128)(2,1)S(1)}, bf16[8,64,128]{2,1,0:T(8,128)(2,1)S(1)}, bf16[8,64,128]{2,1,0:T(8,128)(2,1)S(1)}, f32[8,64,128]{2,1,0:T...) custom-call(s32[1,8]{1,0:T(1,128)} %bitcast.27, s32[1,8]{1,0:T(1,128)} %bitcast.20, f32[8,2,26]{2,1,0:T(2,128)} %couple_far.1, ...), custom_call_target="tpu_custom_call" | custom-call | flops 100000000 | bytes 3000000 | tf_op jit(solution)/shard_map/prepare/pallas_call | solution.py:374
  13.2 0.0 all-to-all-done
  13.2 0.2 gather.1
  13.4 16.8 %all_to_all.15 = bf16[16,128,128]{2,1,0:T(8,128)(2,1)S(1)} all-to-all(bf16[16,128,128]{2,1,0:T(8,128)(2,1)S(1)} %gather.1), channel_id=1, replica_groups={{11,13,15,1,2,3,7,14,6,9,5,12,8,4,10,0},{27,29,31,17,18,19,23,30,22,25,..., dimensions={0} | all-to-all | bytes 1048576 | tf_op jit(solution)/shard_map/all_to_all | solution.py:351
  30.2 1.1 %image.1 = (f32[8,64,128]{2,1,0:T(8,128)S(1)}, bf16[8,128,128]{2,1,0:T(8,128)(2,1)S(1)}, f32[16,128]{1,0:T(8,128)S(1)}) custom-call(s32[1,8]{1,0:T(1,128)S(1)} %get-tuple-element.12.slot, f32[8,1]{1,0:T(8,128)S(1)} %get-tuple-element.13.norm, bf16[32,64,128]{2,1,0:T(8,128)(2,1)S(1)} %bitcast.16, bf16[8,64,128]{2,1,0:T(8,128)(2,1)S(1)} %get-tuple-element.15.lcomb, ...), custom_call_target="tpu_custom_call" | custom-call | tf_op jit(solution)/shard_map/image/pallas_call | solution.py:409
  31.3 8.1 %all_to_all.16 = f32[16,1,128]{2,1,0:T(1,128)S(1)} all-to-all(f32[16,1,128]{2,1,0:T(1,128)S(1)} %bitcast.19), channel_id=1, replica_groups={{11,13,15,1,2,3,7,14,6,9,5,12,8,4,10,0},{27,29,31,17,18,19,23,30,22,25,..., dimensions={0} | all-to-all | bytes 16384 | tf_op jit(solution)/shard_map/all_to_all | solution.py:351
  39.4 1.3 %second.1 = (f32[8,4096]{1,0:T(8,128)}, bf16[8,4096]{1,0:T(8,128)(2,1)}, f32[3]{0:T(128)}) custom-call(f32[16,128]{1,0:T(8,128)S(1)} %bitcast.18, f32[8,64,128]{2,1,0:T(8,128)S(1)} %get-tuple-element.19.hpsi, f32[8,64,128]{2,1,0:T(8,128)S(1)} %get-tuple-element.17.wave, bf16[8,128,128]{2,1,0:T(8,128)(2,1)S(1)} %get-tuple-element.20.rsel, ...), custom_call_target="tpu_custom_call" | custom-call | tf_op jit(solution)/shard_map/second/pallas_call | solution.py:429
Async XLA Ops:
  0.6 0.7 %copy-start.2 = (s32[8]{0:T(128)S(1)}, s32[8]{0:T(128)}, u32[]{:S(2)}) copy-start(s32[8]{0:T(128)} %param.14) | copy-start | bytes 100
  0.6 0.7 %copy-start = (s32[8,1]{0,1:T(1,128)S(1)}, s32[8,1]{0,1:T(1,128)}, u32[]{:S(2)}) copy-start(s32[8,1]{0,1:T(1,128)} %param.13) | copy-start | bytes 100
  0.7 0.7 %copy-start.1 = (s32[8,2]{0,1:T(2,128)S(1)}, s32[8,2]{0,1:T(2,128)}, u32[]{:S(2)}) copy-start(s32[8,2]{0,1:T(2,128)} %param.15) | copy-start | bytes 196
  2.1 11.1 %all-to-all-start = ((s32[16,1,4]{2,1,0:T(1,128)}), s32[16,1,4]{2,1,0:T(1,128)S(1)}, u32[]{:S(2)}, u32[]{:S(2)}) async-start(s32[16,1,4]{2,1,0:T(1,128)} %bitcast.13), calls=%async_computation | async-start | bytes 16384 | tf_op jit(solution)/shard_map/all_to_all | solution.py:351

commit v9 on v8

--- a/solution.py
+++ b/solution.py
@@ -15,6 +15,7 @@
 SPACE = 16
 TINY = 1e-30
 ORDER = (11, 13, 15, 1, 2, 3, 7, 14, 6, 9, 5, 12, 8, 4, 10, 0)
+SUM_ORDER = (11, 8, 14, 0, 9, 2, 6, 7, 5, 3, 12, 4, 1, 10, 13, 15)
 F32 = jnp.float32
 BF16 = jnp.bfloat16
 
@@ -35,9 +36,9 @@
     return 0 if peers % len(ORDER) else peers // len(ORDER)
 
 
-def listed(peers):
+def listed(peers, order):
     run = run_of(peers)
-    return [q * run + i for q in ORDER for i in range(run)] if run else list(range(peers))
+    return [q * run + i for q in order for i in range(run)] if run else list(range(peers))
 
 
 def replaced(values, pairs, peers):
@@ -346,8 +347,8 @@
     groups = blocks // 8
     of = jax.ShapeDtypeStruct
 
-    def exchange(values):
-        members = [listed(peers)]
+    def exchange(values, order=ORDER):
+        members = [listed(peers, order)]
         return lax.all_to_all(values, "sec", split_axis=0, concat_axis=0, axis_index_groups=members, tiled=True)
 
     owner = right_owner.T
@@ -424,7 +425,7 @@
         compiler_params=params(24),
         name="image",
     )(slot, norm, received, lcomb, image, wave)
-    stats = exchange(stats.reshape(peers, groups, LANES)).reshape(peers * groups, LANES)
+    stats = exchange(stats.reshape(peers, groups, LANES), SUM_ORDER).reshape(peers * groups, LANES)
 
     second, direction, projected = pl.pallas_call(
         functools.partial(second_kernel, float(blocks * peers * B * B)),

time: 41 us -> 41 us (level)
  no operation moved by 1% of the time
where the time goes in v9:
time: 41 us; the launch traced here: 40.7 us
  blocking collectives  24.9 us (61%)
  starting transfers between devices  7.79 us (19%)
  Pallas kernels  6.63 us (16%)
  local copies, waits for them, and re-layouts  0.69 us (2%)
  between operations  0.68 us (2%)
    all_to_all x2, blocking collectives, exchange(): lax.all_to_all(values, 'sec', split_axis=0, concat_axis=0, axis_index_gro...  24.9 us
    all_to_all x1, starting transfers between devices, exchange(): lax.all_to_all(values, 'sec', split_axis=0, concat_axis=0, axis_index_gro...  7.79 us
    pallas_call x1, Pallas kernels, per_device(): pl.pallas_call(functools.partial(prepare_kernel, peers), out_shape=(of((c...  3.33 us
    pallas_call x1, Pallas kernels, per_device(): pl.pallas_call(functools.partial(second_kernel, float(blocks * peers * B...  1.31 us
    pallas_call x1, Pallas kernels, per_device(): pl.pallas_call(image_kernel, out_shape=(of((blocks, B, LANES), F32), of((...  1.11 us
  transfers between devices with their start and end apart: 1, of which 0 were waited for; matrix products, arithmetic and copies ran while one was open for 0% of the time, Pallas kernels for 8%

profile of v9, /device:TPU:0, one launch (start us, length us, event | category | flops | bytes accessed | tf_op | source)
XLA Modules:
  0.0 40.7 jit_solution(5993961233272526698)
XLA Ops:
  0.6 0.0 copy-start.2
  0.6 0.0 copy-start
  0.7 0.0 copy-start.1
  0.7 0.6 %copy-done.2 = s32[8]{0:T(128)S(1)} copy-done((s32[8]{0:T(128)S(1)}, s32[8]{0:T(128)}, u32[]{:S(2)}) %copy-start.2) | copy-done | bytes 56
  1.3 0.0 copy-done
  1.3 0.0 copy-done.1
  1.3 0.7 %request.1 = s32[16,4]{1,0:T(8,128)} custom-call(s32[1,8]{1,0:T(1,128)S(1)} %bitcast.21, s32[1,8]{1,0:T(1,128)S(1)} %bitcast.23, s32[2,8]{1,0:T(2,128)S(1)} %bitcast.22), custom_call_target="tpu_custom_call" | custom-call | tf_op jit(solution)/shard_map/request/pallas_call | solution.py:355
  2.1 7.8 %all-to-all-start = ((s32[16,1,4]{2,1,0:T(1,128)}), s32[16,1,4]{2,1,0:T(1,128)S(1)}, u32[]{:S(2)}, u32[]{:S(2)}) async-start(s32[16,1,4]{2,1,0:T(1,128)} %bitcast.13), calls=%async_computation | async-start | bytes 16384 | tf_op jit(solution)/shard_map/all_to_all | solution.py:352
  9.8 3.3 %prepare.1 = (bf16[104,32,128]{2,1,0:T(8,128)(2,1)S(1)}, bf16[8,64,128]{2,1,0:T(8,128)(2,1)S(1)}, bf16[8,64,128]{2,1,0:T(8,128)(2,1)S(1)}, f32[8,64,128]{2,1,0:T...) custom-call(s32[1,8]{1,0:T(1,128)} %bitcast.27, s32[1,8]{1,0:T(1,128)} %bitcast.20, f32[8,2,26]{2,1,0:T(2,128)} %couple_far.1, ...), custom_call_target="tpu_custom_call" | custom-call | flops 100000000 | bytes 3000000 | tf_op jit(solution)/shard_map/prepare/pallas_call | solution.py:375
  13.2 0.0 all-to-all-done
  13.2 0.2 gather.1
  13.4 16.8 %all_to_all.15 = bf16[16,128,128]{2,1,0:T(8,128)(2,1)S(1)} all-to-all(bf16[16,128,128]{2,1,0:T(8,128)(2,1)S(1)} %gather.1), channel_id=1, replica_groups={{11,13,15,1,2,3,7,14,6,9,5,12,8,4,10,0},{27,29,31,17,18,19,23,30,22,25,..., dimensions={0} | all-to-all | bytes 1048576 | tf_op jit(solution)/shard_map/all_to_all | solution.py:352
  30.2 1.1 %image.1 = (f32[8,64,128]{2,1,0:T(8,128)S(1)}, bf16[8,128,128]{2,1,0:T(8,128)(2,1)S(1)}, f32[16,128]{1,0:T(8,128)S(1)}) custom-call(s32[1,8]{1,0:T(1,128)S(1)} %get-tuple-element.12.slot, f32[8,1]{1,0:T(8,128)S(1)} %get-tuple-element.13.norm, bf16[32,64,128]{2,1,0:T(8,128)(2,1)S(1)} %bitcast.16, bf16[8,64,128]{2,1,0:T(8,128)(2,1)S(1)} %get-tuple-element.15.lcomb, ...), custom_call_target="tpu_custom_call" | custom-call | tf_op jit(solution)/shard_map/image/pallas_call | solution.py:410
  31.3 8.1 %all_to_all.16 = f32[16,1,128]{2,1,0:T(1,128)S(1)} all-to-all(f32[16,1,128]{2,1,0:T(1,128)S(1)} %bitcast.19), channel_id=1, replica_groups={{11,8,14,0,9,2,6,7,5,3,12,4,1,10,13,15},{27,24,30,16,25,18,22,23,21,19,..., dimensions={0} | all-to-all | bytes 16384 | tf_op jit(solution)/shard_map/all_to_all | solution.py:352
  39.4 1.3 %second.1 = (f32[8,4096]{1,0:T(8,128)}, bf16[8,4096]{1,0:T(8,128)(2,1)}, f32[3]{0:T(128)}) custom-call(f32[16,128]{1,0:T(8,128)S(1)} %bitcast.18, f32[8,64,128]{2,1,0:T(8,128)S(1)} %get-tuple-element.19.hpsi, f32[8,64,128]{2,1,0:T(8,128)S(1)} %get-tuple-element.17.wave, bf16[8,128,128]{2,1,0:T(8,128)(2,1)S(1)} %get-tuple-element.20.rsel, ...), custom_call_target="tpu_custom_call" | custom-call | tf_op jit(solution)/shard_map/second/pallas_call | solution.py:430
Async XLA Ops:
  0.6 0.7 %copy-start.2 = (s32[8]{0:T(128)S(1)}, s32[8]{0:T(128)}, u32[]{:S(2)}) copy-start(s32[8]{0:T(128)} %param.14) | copy-start | bytes 100
  0.6 0.7 %copy-start = (s32[8,1]{0,1:T(1,128)S(1)}, s32[8,1]{0,1:T(1,128)}, u32[]{:S(2)}) copy-start(s32[8,1]{0,1:T(1,128)} %param.13) | copy-start | bytes 100
  0.7 0.7 %copy-start.1 = (s32[8,2]{0,1:T(2,128)S(1)}, s32[8,2]{0,1:T(2,128)}, u32[]{:S(2)}) copy-start(s32[8,2]{0,1:T(2,128)} %param.15) | copy-start | bytes 196
  2.1 11.1 %all-to-all-start = ((s32[16,1,4]{2,1,0:T(1,128)}), s32[16,1,4]{2,1,0:T(1,128)S(1)}, u32[]{:S(2)}, u32[]{:S(2)}) async-start(s32[16,1,4]{2,1,0:T(1,128)} %bitcast.13), calls=%async_computation | async-start | bytes 16384 | tf_op jit(solution)/shard_map/all_to_all | solution.py:352

commit v10 on v9

--- a/solution.py
+++ b/solution.py
@@ -301,6 +301,14 @@
 
     each(blocks, move)
 
+    def rows(source, target, g):
+        place = pl.ds(pl.multiple_of(8 * g, 8), 8)
+        for t in range(TILES):
+            tile = source[pl.ds(pl.multiple_of((g * TILES + t) * 8, 8), 8), :]
+            target[place, t * LANES : (t + 1) * LANES] = tile.astype(target.dtype)
+
+    each(blocks // 8, functools.partial(rows, steps, direction))
+
     def apply(k):
         zed[k, 0:B] = dot(narrow[k], rsel[k, 0:B]).astype(BF16)
         zed[k, B : 2 * B] = dot(narrow[k], rsel[k, B : 2 * B]).astype(BF16)
@@ -312,14 +320,7 @@
 
     each(blocks, close)
 
-    def rows(g):
-        place = pl.ds(pl.multiple_of(8 * g, 8), 8)
-        for source, target in ((steps, direction), (stage, second)):
-            for t in range(TILES):
-                tile = source[pl.ds(pl.multiple_of((g * TILES + t) * 8, 8), 8), :]
-                target[place, t * LANES : (t + 1) * LANES] = tile.astype(target.dtype)
-
-    each(blocks // 8, rows)
+    each(blocks // 8, functools.partial(rows, stage, second))
     projected[0] = theta[0, 0]
     projected[1] = jnp.sqrt(spread)[0, 0]
     projected[2] = (along / rr)[0, 0]

time: 41 us -> 41 us (level)
  no operation moved by 1% of the time
where the time goes in v10:
time: 41 us; the launch traced here: 40.7 us
  blocking collectives  24.9 us (61%)
  starting transfers between devices  7.79 us (19%)
  Pallas kernels  6.63 us (16%)
  local copies, waits for them, and re-layouts  0.69 us (2%)
  between operations  0.68 us (2%)
    all_to_all x2, blocking collectives, exchange(): lax.all_to_all(values, 'sec', split_axis=0, concat_axis=0, axis_index_gro...  24.9 us
    all_to_all x1, starting transfers between devices, exchange(): lax.all_to_all(values, 'sec', split_axis=0, concat_axis=0, axis_index_gro...  7.79 us
    pallas_call x1, Pallas kernels, per_device(): pl.pallas_call(functools.partial(prepare_kernel, peers), out_shape=(of((c...  3.33 us
    pallas_call x1, Pallas kernels, per_device(): pl.pallas_call(functools.partial(second_kernel, float(blocks * peers * B...  1.31 us
    pallas_call x1, Pallas kernels, per_device(): pl.pallas_call(image_kernel, out_shape=(of((blocks, B, LANES), F32), of((...  1.11 us
  transfers between devices with their start and end apart: 1, of which 0 were waited for; matrix products, arithmetic and copies ran while one was open for 0% of the time, Pallas kernels for 8%

profile of v10, /device:TPU:0, one launch (start us, length us, event | category | flops | bytes accessed | tf_op | source)
XLA Modules:
  0.0 40.7 jit_solution(5993961233272526698)
XLA Ops:
  0.6 0.0 copy-start.2
  0.6 0.0 copy-start
  0.7 0.0 copy-start.1
  0.7 0.6 %copy-done.2 = s32[8]{0:T(128)S(1)} copy-done((s32[8]{0:T(128)S(1)}, s32[8]{0:T(128)}, u32[]{:S(2)}) %copy-start.2) | copy-done | bytes 56
  1.3 0.0 copy-done
  1.3 0.0 copy-done.1
  1.3 0.7 %request.1 = s32[16,4]{1,0:T(8,128)} custom-call(s32[1,8]{1,0:T(1,128)S(1)} %bitcast.21, s32[1,8]{1,0:T(1,128)S(1)} %bitcast.23, s32[2,8]{1,0:T(2,128)S(1)} %bitcast.22), custom_call_target="tpu_custom_call" | custom-call | tf_op jit(solution)/shard_map/request/pallas_call | solution.py:356
  2.1 7.8 %all-to-all-start = ((s32[16,1,4]{2,1,0:T(1,128)}), s32[16,1,4]{2,1,0:T(1,128)S(1)}, u32[]{:S(2)}, u32[]{:S(2)}) async-start(s32[16,1,4]{2,1,0:T(1,128)} %bitcast.13), calls=%async_computation | async-start | bytes 16384 | tf_op jit(solution)/shard_map/all_to_all | solution.py:353
  9.8 3.3 %prepare.1 = (bf16[104,32,128]{2,1,0:T(8,128)(2,1)S(1)}, bf16[8,64,128]{2,1,0:T(8,128)(2,1)S(1)}, bf16[8,64,128]{2,1,0:T(8,128)(2,1)S(1)}, f32[8,64,128]{2,1,0:T...) custom-call(s32[1,8]{1,0:T(1,128)} %bitcast.27, s32[1,8]{1,0:T(1,128)} %bitcast.20, f32[8,2,26]{2,1,0:T(2,128)} %couple_far.1, ...), custom_call_target="tpu_custom_call" | custom-call | flops 100000000 | bytes 3000000 | tf_op jit(solution)/shard_map/prepare/pallas_call | solution.py:376
  13.2 0.0 all-to-all-done
  13.2 0.2 gather.1
  13.4 16.8 %all_to_all.15 = bf16[16,128,128]{2,1,0:T(8,128)(2,1)S(1)} all-to-all(bf16[16,128,128]{2,1,0:T(8,128)(2,1)S(1)} %gather.1), channel_id=1, replica_groups={{11,13,15,1,2,3,7,14,6,9,5,12,8,4,10,0},{27,29,31,17,18,19,23,30,22,25,..., dimensions={0} | all-to-all | bytes 1048576 | tf_op jit(solution)/shard_map/all_to_all | solution.py:353
  30.2 1.1 %image.1 = (f32[8,64,128]{2,1,0:T(8,128)S(1)}, bf16[8,128,128]{2,1,0:T(8,128)(2,1)S(1)}, f32[16,128]{1,0:T(8,128)S(1)}) custom-call(s32[1,8]{1,0:T(1,128)S(1)} %get-tuple-element.12.slot, f32[8,1]{1,0:T(8,128)S(1)} %get-tuple-element.13.norm, bf16[32,64,128]{2,1,0:T(8,128)(2,1)S(1)} %bitcast.16, bf16[8,64,128]{2,1,0:T(8,128)(2,1)S(1)} %get-tuple-element.15.lcomb, ...), custom_call_target="tpu_custom_call" | custom-call | tf_op jit(solution)/shard_map/image/pallas_call | solution.py:411
  31.3 8.1 %all_to_all.16 = f32[16,1,128]{2,1,0:T(1,128)S(1)} all-to-all(f32[16,1,128]{2,1,0:T(1,128)S(1)} %bitcast.19), channel_id=1, replica_groups={{11,8,14,0,9,2,6,7,5,3,12,4,1,10,13,15},{27,24,30,16,25,18,22,23,21,19,..., dimensions={0} | all-to-all | bytes 16384 | tf_op jit(solution)/shard_map/all_to_all | solution.py:353
  39.4 1.3 %second.1 = (f32[8,4096]{1,0:T(8,128)}, bf16[8,4096]{1,0:T(8,128)(2,1)}, f32[3]{0:T(128)}) custom-call(f32[16,128]{1,0:T(8,128)S(1)} %bitcast.18, f32[8,64,128]{2,1,0:T(8,128)S(1)} %get-tuple-element.19.hpsi, f32[8,64,128]{2,1,0:T(8,128)S(1)} %get-tuple-element.17.wave, bf16[8,128,128]{2,1,0:T(8,128)(2,1)S(1)} %get-tuple-element.20.rsel, ...), custom_call_target="tpu_custom_call" | custom-call | tf_op jit(solution)/shard_map/second/pallas_call | solution.py:431
Async XLA Ops:
  0.6 0.7 %copy-start.2 = (s32[8]{0:T(128)S(1)}, s32[8]{0:T(128)}, u32[]{:S(2)}) copy-start(s32[8]{0:T(128)} %param.14) | copy-start | bytes 100
  0.6 0.7 %copy-start = (s32[8,1]{0,1:T(1,128)S(1)}, s32[8,1]{0,1:T(1,128)}, u32[]{:S(2)}) copy-start(s32[8,1]{0,1:T(1,128)} %param.13) | copy-start | bytes 100
  0.7 0.7 %copy-start.1 = (s32[8,2]{0,1:T(2,128)S(1)}, s32[8,2]{0,1:T(2,128)}, u32[]{:S(2)}) copy-start(s32[8,2]{0,1:T(2,128)} %param.15) | copy-start | bytes 196
  2.1 11.1 %all-to-all-start = ((s32[16,1,4]{2,1,0:T(1,128)}), s32[16,1,4]{2,1,0:T(1,128)S(1)}, u32[]{:S(2)}, u32[]{:S(2)}) async-start(s32[16,1,4]{2,1,0:T(1,128)} %bitcast.13), calls=%async_computation | async-start | bytes 16384 | tf_op jit(solution)/shard_map/all_to_all | solution.py:353
